TPU v7x, 32 devices: a whole 2x2x4 slice. The times are simulated.
32 devices in a mesh: space: 8 (over y, x, core), chan: 4 (over z).
Axes of the slice: x: 2, y: 2, z: 4, core: 2. Of those that a mesh axis runs over, the one named last changes fastest.
Arguments:
- volume: bfloat16 [128, 8, 64, 128], P('chan', 'space'), may hold values from -6 to 6
- weight_one: bfloat16 [27, 128, 128], replicated, may hold values from -0.109375 to 0.109375
- bias_one: float32 [128], replicated, may hold values from -3 to 3
- weight_two: bfloat16 [27, 128, 128], replicated, may hold values from -0.109375 to 0.109375
- bias_two: float32 [128], replicated, may hold values from -3 to 3
Outputs:
- features: bfloat16 [128, 8, 64, 128], P('chan', 'space')
All inputs are finite; a program needn't handle non-finite values.
Results may differ from a plain program's by a relative error of at most 0.0045.
Values may be sent and summed in bfloat16 or wider, within the bound.
A program may use at most 64 MiB of HBM per device.

v0:
```python
import jax
import jax.numpy as jnp
from jax import lax
from jax.sharding import PartitionSpec as P


def extended(array, sides, width):
    for axis, dim in sides:
        count, length = (lax.axis_size(axis), array.shape[dim])
        up = [(i, (i + 1) % count) for i in range(count - 1)]
        down = [(j, i) for i, j in up]
        last = lax.slice_in_dim(array, length - width, length, axis=dim)
        initial = lax.slice_in_dim(array, 0, width, axis=dim)
        before = lax.ppermute(last, axis, up)
        after = lax.ppermute(initial, axis, down)
        array = jnp.concatenate([before, array, after], axis=dim)
    return array


def convolve(rimmed, kernel, planes):
    rows_out = rimmed.shape[2]
    depth = rimmed.shape[3]
    summed = None
    for shift_x in range(3):
        slab_in = rimmed[:, shift_x : shift_x + planes]
        tap_weights = kernel[9 * shift_x : 9 * shift_x + 9]
        products = jnp.einsum(
            "tio,ixyz->toxyz", tap_weights, slab_in, preferred_element_type=jnp.float32
        )
        padded = jnp.pad(products, ((0, 0), (0, 0), (0, 0), (1, 1), (1, 1)))
        for shift_y in range(3):
            for shift_z in range(3):
                term = padded[
                    3 * shift_y + shift_z,
                    :,
                    :,
                    shift_y : shift_y + rows_out,
                    shift_z : shift_z + depth,
                ]
                summed = term if summed is None else summed + term
    return summed


def per_device(volume, weight_one, bias_one, weight_two, bias_two):
    slices = volume.shape[0]
    planes = volume.shape[1]
    layers = ((weight_one, bias_one), (weight_two, bias_two))
    first_filter = lax.axis_index("chan") * slices
    current = volume
    for kernel, offsets in layers:
        gathered = lax.all_gather(current, "chan", axis=0, tiled=True)
        rimmed = extended(gathered, (("space", 1),), 1)
        own_kernel = lax.dynamic_slice_in_dim(kernel, first_filter, slices, 2)
        own_offsets = lax.dynamic_slice_in_dim(offsets, first_filter, slices, 0)
        summed = convolve(rimmed, own_kernel, planes)
        current = jax.nn.relu(summed + own_offsets[:, None, None, None]).astype(jnp.bfloat16)
    return current


def solution(mesh):
    placed = (P("chan", "space", None, None), P(), P(), P(), P())
    return jax.shard_map(
        per_device,
        mesh=mesh,
        in_specs=placed,
        out_specs=P("chan", "space", None, None),
        check_vma=False,
    )
```

profile of v0, /device:TPU:4, one launch (start us, length us, event | category | flops | bytes accessed | tf_op | source)
XLA Modules:
  0.0 233.6 jit_solution(5128643968124534367)
XLA Ops:
  6.5 2.3 copy.8
  8.8 0.0 all-gather.3.cloned.1.call-update
  8.8 0.0 all-gather.5.cloned.1.call-start
  8.9 47.3 %all-gather.3.cloned.1.call-done = bf16[128,1,64,128]{3,0,2,1:T(8,128)(2,1)} async-done(((bf16[32,1,64,128]{3,0,2,1:T(8,128)(2,1)}), bf16[128,1,64,128]{3,0,2,1:T(8,128)(2,1)}) %all-gather.3.cloned.1.call-update) | async-done | bytes 2097168 | tf_op jit(solution)/shard_map/all_gather | solution.py:51
  56.1 1.9 collective-permute-start
  58.0 4.5 %collective-permute-start.1 = (bf16[128,1,64,128]{3,0,2,1:T(8,128)(2,1)}, bf16[128,1,64,128]{3,0,2,1:T(8,128)(2,1)S(1)}, u32[]{:S(2)}, u32[]{:S(2)}) collective-permute-start(bf16[128,1,64,128]{3,0,2,1:T(8,128)(2,1)} %all-gather.3.cloned.1.call-done), channel_id=1, source_target_pairs={{4,0},{8,4},{12,8},{16,12},{20,16},{24,20},{28,24},{5,1},{9,5},{13... | collective-permute-start | bytes 6291464 | tf_op jit(solution)/shard_map/ppermute | solution.py:15
  62.6 0.7 dynamic_slice.14
  63.3 3.1 %fusion.8 = f32[9,32,64,128]{3,1,2,0:T(8,128)S(1)} fusion(bf16[128,1,64,128]{3,0,2,1:T(8,128)(2,1)} %all-gather.3.cloned.1.call-done, bf16[27,128,128]{2,1,0:T(8,128)(2,1)S(1)} %copy-done, s32[]{:T(128)S(6)} %add.691, s32[]{:T(128)S(6)} %select_n.2), kind=kOutput, calls=%fused_computation.56 | convolution fusion | flops 603979776 | bytes 11829256 | tf_op jit(solution)/shard_map/tio,ixyz->toxyz/dot_general | solution.py:27
  66.5 37.9 %collective-permute-done = bf16[128,1,64,128]{3,0,2,1:T(8,128)(2,1)} collective-permute-done((bf16[128,1,64,128]{3,0,2,1:T(8,128)(2,1)}, bf16[128,1,64,128]{3,0,2,1:T(8,128)(2,1)}, u32[]{:S(2)}, u32[]{:S(2)}) %collective-permute-start) | collective-permute-done | bytes 2097184 | tf_op jit(solution)/shard_map/ppermute | solution.py:14
  104.3 3.1 %fusion.10 = f32[9,32,64,128]{3,1,2,0:T(8,128)S(1)} fusion(bf16[128,1,64,128]{3,0,2,1:T(8,128)(2,1)} %collective-permute-done, bf16[27,128,128]{2,1,0:T(8,128)(2,1)S(1)} %copy-done, s32[]{:T(128)S(6)} %select_n.2), kind=kOutput, calls=%fused_computation.58 | convolution fusion | flops 603979776 | bytes 11829252 | tf_op jit(solution)/shard_map/tio,ixyz->toxyz/dot_general | solution.py:27
  107.4 0.0 collective-permute-done.1
  107.5 4.5 %fusion.6 = f32[9,32,64,128]{3,1,2,0:T(8,128)} fusion(bf16[128,1,64,128]{3,0,2,1:T(8,128)(2,1)S(1)} %collective-permute-done.1, bf16[27,128,128]{2,1,0:T(8,128)(2,1)S(1)} %copy-done, s32[]{:T(128)S(6)} %add.692, s32[]{:T(128)S(6)} %select_n.2), kind=kOutput, calls=%fused_computation.54 | convolution fusion | flops 603979776 | bytes 11829256 | tf_op jit(solution)/shard_map/tio,ixyz->toxyz/dot_general | solution.py:27
  112.0 8.2 %maximum_convert_fusion.1 = bf16[32,1,64,128]{3,0,2,1:T(8,128)(2,1)} fusion(f32[9,32,1,64,128]{4,1,3,2,0:T(8,128)} %bitcast.483, f32[9,32,64,128]{3,1,2,0:T(8,128)} %fusion.6, f32[9,32,1,64,128]{4,1,3,2,0:T(8,128)S(1)} %bitcast.479, f32[9,32,64,128]{3,1,2,0:T(8,128)S(1)} %fusion.8, f32[9,32,1,64,128]{4,1,3,2,0:T(8,128)S(1)} %bitcast.481, ...), kind=kLoop, calls=%fused_computation.159 | loop fusion | flops 7602176 | bytes 31981696 | tf_op jit(solution)/shard_map/convert_element_type | solution.py:56
  120.2 0.0 all-gather.5.cloned.1.call-update
  120.2 43.9 %all-gather.5.cloned.1.call-done = bf16[128,1,64,128]{3,0,2,1:T(8,128)(2,1)} async-done(((bf16[32,1,64,128]{3,0,2,1:T(8,128)(2,1)}), bf16[128,1,64,128]{3,0,2,1:T(8,128)(2,1)}) %all-gather.5.cloned.1.call-update) | async-done | bytes 2097168 | tf_op jit(solution)/shard_map/all_gather | solution.py:51
  164.1 1.9 collective-permute-start.2
  166.0 4.7 %collective-permute-start.3 = (bf16[128,1,64,128]{3,0,2,1:T(8,128)(2,1)}, bf16[128,1,64,128]{3,0,2,1:T(8,128)(2,1)S(1)}, u32[]{:S(2)}, u32[]{:S(2)}) collective-permute-start(bf16[128,1,64,128]{3,0,2,1:T(8,128)(2,1)} %all-gather.5.cloned.1.call-done), channel_id=1, source_target_pairs={{4,0},{8,4},{12,8},{16,12},{20,16},{24,20},{28,24},{5,1},{9,5},{13... | collective-permute-start | bytes 6291464 | tf_op jit(solution)/shard_map/ppermute | solution.py:15
  170.8 0.1 dynamic_slice.15
  170.9 3.1 %fusion.2 = f32[9,32,64,128]{3,1,2,0:T(8,128)S(1)} fusion(bf16[128,1,64,128]{3,0,2,1:T(8,128)(2,1)} %all-gather.5.cloned.1.call-done, bf16[27,128,128]{2,1,0:T(8,128)(2,1)S(1)} %copy-done.2, s32[]{:T(128)S(6)} %add.691, s32[]{:T(128)S(6)} %select_n.2), kind=kOutput, calls=%fused_computation.50 | convolution fusion | flops 603979776 | bytes 11829256 | tf_op jit(solution)/shard_map/tio,ixyz->toxyz/dot_general | solution.py:27
  174.0 38.2 %collective-permute-done.2 = bf16[128,1,64,128]{3,0,2,1:T(8,128)(2,1)S(1)} collective-permute-done((bf16[128,1,64,128]{3,0,2,1:T(8,128)(2,1)}, bf16[128,1,64,128]{3,0,2,1:T(8,128)(2,1)S(1)}, u32[]{:S(2)}, u32[]{:S(2)}) %collective-permute-start.2) | collective-permute-done | bytes 2097184 | tf_op jit(solution)/shard_map/ppermute | solution.py:14
  212.2 1.5 fusion.4
  213.7 4.5 %fusion = f32[9,32,64,128]{3,1,2,0:T(8,128)} fusion(bf16[128,1,64,128]{3,0,2,1:T(8,128)(2,1)S(1)} %collective-permute-done.3, bf16[27,128,128]{2,1,0:T(8,128)(2,1)S(1)} %copy-done.2, s32[]{:T(128)S(6)} %add.692, s32[]{:T(128)S(6)} %select_n.2), kind=kOutput, calls=%fused_computation.48 | convolution fusion | flops 603979776 | bytes 11829256 | tf_op jit(solution)/shard_map/tio,ixyz->toxyz/dot_general | solution.py:27
  218.3 7.5 %maximum_convert_fusion = bf16[32,1,64,128]{3,0,2,1:T(8,128)(2,1)S(1)} fusion(f32[9,32,1,64,128]{4,1,3,2,0:T(8,128)} %bitcast.482, f32[9,32,64,128]{3,1,2,0:T(8,128)} %fusion, f32[9,32,1,64,128]{4,1,3,2,0:T(8,128)S(1)} %bitcast.478, f32[9,32,64,128]{3,1,2,0:T(8,128)S(1)} %fusion.2, f32[9,32,1,64,128]{4,1,3,2,0:T(8,128)S(1)} %bitcast.480, ...), kind=kLoop, calls=%fused_computation.158 | loop fusion | flops 7602176 | bytes 31981696 | tf_op jit(solution)/shard_map/convert_element_type | solution.py:56
  225.8 1.0 copy.9
  (10 shorter events, 0.0 us)
Async XLA Ops:
  6.5 56.8 %copy-start = (bf16[27,128,128]{2,1,0:T(8,128)(2,1)S(1)}, bf16[27,128,128]{2,1,0:T(8,128)(2,1)}, u32[]{:S(2)}) copy-start(bf16[27,128,128]{2,1,0:T(8,128)(2,1)} %param.6) | copy-start | bytes 2654212
  6.5 49.6 %all-gather.3.cloned.1.call-start = ((), (), s32[]{:S(2)}) async-start(), calls=%async_computation | async-start | bytes 2621440 | tf_op jit(solution)/shard_map/all_gather | solution.py:51
  8.8 155.3 %all-gather.5.cloned.1.call-start = ((), (), s32[]{:S(2)}) async-start(), calls=%async_computation.1 | async-start | bytes 2621440 | tf_op jit(solution)/shard_map/all_gather | solution.py:51
  56.1 48.2 %collective-permute-start = (bf16[128,1,64,128]{3,0,2,1:T(8,128)(2,1)}, bf16[128,1,64,128]{3,0,2,1:T(8,128)(2,1)}, u32[]{:S(2)}, u32[]{:S(2)}) collective-permute-start(bf16[128,1,64,128]{3,0,2,1:T(8,128)(2,1)} %all-gather.3.cloned.1.call-done), channel_id=1, source_target_pairs={{0,4},{4,8},{8,12},{12,16},{16,20},{20,24},{24,28},{1,5},{5,9},{9,... | collective-permute-start | bytes 6291464 | tf_op jit(solution)/shard_map/ppermute | solution.py:14
  58.0 49.4 %collective-permute-start.1 = (bf16[128,1,64,128]{3,0,2,1:T(8,128)(2,1)}, bf16[128,1,64,128]{3,0,2,1:T(8,128)(2,1)S(1)}, u32[]{:S(2)}, u32[]{:S(2)}) collective-permute-start(bf16[128,1,64,128]{3,0,2,1:T(8,128)(2,1)} %all-gather.3.cloned.1.call-done), channel_id=1, source_target_pairs={{4,0},{8,4},{12,8},{16,12},{20,16},{24,20},{28,24},{5,1},{9,5},{13... | collective-permute-start | bytes 6291464 | tf_op jit(solution)/shard_map/ppermute | solution.py:15
  112.0 58.8 %copy-start.3 = (f32[128]{0:T(128)S(1)}, f32[128]{0:T(128)}, u32[]{:S(2)}) copy-start(f32[128]{0:T(128)} %param.9) | copy-start | bytes 1540
  112.0 58.9 %copy-start.2 = (bf16[27,128,128]{2,1,0:T(8,128)(2,1)S(1)}, bf16[27,128,128]{2,1,0:T(8,128)(2,1)}, u32[]{:S(2)}) copy-start(bf16[27,128,128]{2,1,0:T(8,128)(2,1)} %param.8) | copy-start | bytes 2654212
  164.1 48.1 %collective-permute-start.2 = (bf16[128,1,64,128]{3,0,2,1:T(8,128)(2,1)}, bf16[128,1,64,128]{3,0,2,1:T(8,128)(2,1)S(1)}, u32[]{:S(2)}, u32[]{:S(2)}) collective-permute-start(bf16[128,1,64,128]{3,0,2,1:T(8,128)(2,1)} %all-gather.5.cloned.1.call-done), channel_id=1, source_target_pairs={{0,4},{4,8},{8,12},{12,16},{16,20},{20,24},{24,28},{1,5},{5,9},{9,... | collective-permute-start | bytes 6291464 | tf_op jit(solution)/shard_map/ppermute | solution.py:14
  166.0 47.7 %collective-permute-start.3 = (bf16[128,1,64,128]{3,0,2,1:T(8,128)(2,1)}, bf16[128,1,64,128]{3,0,2,1:T(8,128)(2,1)S(1)}, u32[]{:S(2)}, u32[]{:S(2)}) collective-permute-start(bf16[128,1,64,128]{3,0,2,1:T(8,128)(2,1)} %all-gather.5.cloned.1.call-done), channel_id=1, source_target_pairs={{4,0},{8,4},{12,8},{16,12},{20,16},{24,20},{28,24},{5,1},{9,5},{13... | collective-permute-start | bytes 6291464 | tf_op jit(solution)/shard_map/ppermute | solution.py:15
  218.3 8.5 %copy-start.1 = (bf16[27,128,128]{2,1,0:T(8,128)(2,1)S(1)}, bf16[27,128,128]{2,1,0:T(8,128)(2,1)}, u32[]{:S(2)}) copy-start(bf16[27,128,128]{2,1,0:T(8,128)(2,1)} %param.6) | copy-start | bytes 2654212
Sparse Core Ops, SparseCore 0:
  8.9 47.1 all-gather.2
  120.3 43.7 all-gather.4
where the time goes:
time: 236 us; the launch traced here: 234 us
  waiting for transfers between devices  167 us (71%)
  matrix products  20 us (8%)
  other arithmetic  15.7 us (7%)
  between operations  13.5 us (6%)
  starting transfers between devices  13.1 us (6%)
  local copies, waits for them, and re-layouts  4.08 us (2%)
    all_gather x2, waiting for transfers between devices, per_device(): gathered = lax.all_gather(current, 'chan', axis=0, tiled=True)  91.2 us
    ppermute x2, waiting for transfers between devices, extended(): before = lax.ppermute(last, axis, up)  76.1 us
    dot_general x6, matrix products, convolve(): jnp.einsum('tio,ixyz->toxyz', tap_weights, slab_in, preferred_element_typ...  20 us
    convert_element_type x2, other arithmetic, per_device(): jax.nn.relu(summed + own_offsets[:, None, None, None]).astype(jnp.bfloat16)  15.7 us
    ppermute x2, starting transfers between devices, extended(): after = lax.ppermute(initial, axis, down)  9.26 us
  transfers between devices with their start and end apart: 6, of which 4 were waited for; matrix products, arithmetic and copies ran while one was open for 5% of the time, Pallas kernels for 0%

commit v1 on v0

v1 whole, which is shorter than its diff:
```python
import functools

import jax
import jax.numpy as jnp
from jax import lax
from jax.experimental import pallas as pl
from jax.experimental.pallas import tpu as pltpu
from jax.sharding import PartitionSpec as P

MESH = pl.DeviceIdType.MESH
BF16 = jnp.bfloat16
F32 = jnp.float32
GROUPS = 4
ORDER_ONE = (0, 1, 3, 2)
ORDER_TWO = (0, 1, 2, 3)


def kernel(ns, nc, rows, depth, own, vol, w1, b1, w2, b2, out,
           field, hidden, result, raw1, raw2, mat1, mat2, bias,
           w_sem, local_sem, z_send, z_recv, x_send, x_recv,
           h_send, h_recv, e_send, e_recv, o_send, o_recv, o_local):
    s = lax.axis_index("space")
    c = lax.axis_index("chan")
    chans = own * nc
    has_lo, has_hi = s > 0, s < ns - 1
    c_lo, c_hi = c > 0, c < nc - 1
    s_dn, s_up = jnp.maximum(s - 1, 0), jnp.minimum(s + 1, ns - 1)
    c_dn, c_up = jnp.maximum(c - 1, 0), jnp.minimum(c + 1, nc - 1)
    peers = [lax.rem(c + k, nc) for k in range(nc)]
    sources = [lax.rem(c + nc - k, nc) for k in range(nc)]
    width = rows * depth
    wide = width + 2 * depth
    group_rows = rows // GROUPS
    group = group_rows * depth
    cut = (rows // 2 + 2) * depth
    halves = ((0, cut), (cut, wide - cut))

    load1 = pltpu.make_async_copy(w1, raw1, w_sem.at[0])
    load2 = pltpu.make_async_copy(w2, raw2, w_sem.at[1])
    load1.start()
    load2.start()

    @pl.when(s == 0)
    def _():
        field[0] = jnp.zeros((chans, wide), BF16)
        hidden[0] = jnp.zeros((chans, wide), BF16)

    @pl.when(s == ns - 1)
    def _():
        field[2] = jnp.zeros((chans, wide), BF16)
        hidden[2] = jnp.zeros((chans, wide), BF16)

    @pl.when(c == 0)
    def _():
        hidden[:, :, 0:depth] = jnp.zeros((3, chans, depth), BF16)

    @pl.when(c == nc - 1)
    def _():
        hidden[:, :, wide - depth : wide] = jnp.zeros((3, chans, depth), BF16)

    barrier = pltpu.get_barrier_semaphore()

    def greet(space, chan):
        pl.semaphore_signal(barrier, inc=1, device_id=(space, chan), device_id_type=MESH)

    for k in range(1, nc):
        greet(s, peers[k])
    for there, space in ((has_lo, s_dn), (has_hi, s_up)):
        @pl.when(there)
        def _(space=space):
            greet(space, c)

        @pl.when(there & c_lo)
        def _(space=space):
            greet(space, c_dn)

        @pl.when(there & c_hi)
        def _(space=space):
            greet(space, c_up)
    sides = has_lo.astype(jnp.int32) + has_hi.astype(jnp.int32)
    edges = c_lo.astype(jnp.int32) + c_hi.astype(jnp.int32)
    pl.semaphore_wait(barrier, nc - 1 + sides * (1 + edges))

    def part(index):
        return pl.ds(pl.multiple_of(index * own, own), own)

    def window(index, half):
        start, size = halves[half]
        return pl.ds(pl.multiple_of(index * width + start, depth), size)

    def landed(half):
        start, size = halves[half]
        return pl.ds(start, size)

    local = [pltpu.make_async_copy(
        vol.at[:, window(c, h)], field.at[1, part(c), landed(h)], local_sem.at[h])
        for h in range(2)]
    to_z = {(k, h): pltpu.make_async_remote_copy(
        src_ref=vol.at[:, window(peers[k], h)],
        dst_ref=field.at[1, part(c), landed(h)],
        send_sem=z_send.at[k - 1, h], recv_sem=z_recv.at[k - 1, h],
        device_id=(s, peers[k]), device_id_type=MESH)
        for h in range(2) for k in range(1, nc)}
    ways = ((0, has_hi, has_lo, s_up, 0), (1, has_lo, has_hi, s_dn, 2))
    to_x = {}
    for d, _, _, space, plane in ways:
        for h in range(2):
            for k in range(nc):
                if k == 0:
                    src = vol.at[:, window(c, h)]
                else:
                    src = field.at[1, part(sources[k]), landed(h)]
                to_x[d, k, h] = pltpu.make_async_remote_copy(
                    src_ref=src,
                    dst_ref=field.at[plane, part(sources[k]), landed(h)],
                    send_sem=x_send.at[d, k, h], recv_sem=x_recv.at[d, k, h],
                    device_id=(space, c), device_id_type=MESH)

    def forward(k, h):
        for d, sends, _, _, _ in ways:
            @pl.when(sends)
            def _(d=d):
                to_x[d, k, h].start()

    for h in range(2):
        for k in range(1, nc):
            to_z[k, h].start()
        local[h].start()
        forward(0, h)

    def turn(raw, mat):
        for ae in range(9):
            for f in range(3):
                mat[f * chans : (f + 1) * chans, ae * chans : (ae + 1) * chans] = raw[3 * ae + f].T

    load1.wait()
    turn(raw1, mat1)
    bias[0] = jnp.broadcast_to(b1[...], (depth, chans)).T
    bias[1] = jnp.broadcast_to(b2[...], (depth, chans)).T

    for k in range(1, nc):
        to_z[k, 0].wait_recv()
        forward(k, 0)
    load2.wait()
    turn(raw2, mat2)
    for k in range(1, nc):
        to_z[k, 1].wait_recv()
        forward(k, 1)

    lane = lax.broadcasted_iota(jnp.int32, (chans, depth), 1)

    def layer(source, mat, layer_bias, g, store):
        @pl.loop(0, group_rows // 2)
        def _(i):
            at = pl.multiple_of(g * group + i * 2 * depth, 2 * depth)
            stacked = jnp.concatenate(
                [source[a, :, pl.ds(pl.multiple_of(at + e * depth, depth), 2 * depth)]
                 for a in range(3) for e in range(3)], axis=0)
            products = jnp.dot(mat[...], stacked, preferred_element_type=F32)
            for r in range(2):
                cols = slice(r * depth, (r + 1) * depth)
                left = pltpu.roll(products[0:chans, cols], 1, 1)
                right = pltpu.roll(products[2 * chans : 3 * chans, cols], depth - 1, 1)
                total = products[chans : 2 * chans, cols] + layer_bias
                total = total + jnp.where(lane == 0, 0.0, left)
                total = total + jnp.where(lane == depth - 1, 0.0, right)
                store(at + r * depth, jnp.maximum(total, 0.0).astype(BF16))

    def keep(at, value):
        hidden[1, :, pl.ds(pl.multiple_of(at + depth, depth), depth)] = value

    def finish(at, value):
        result[:, pl.ds(pl.multiple_of(at, depth), depth)] = value

    to_h = {(d, g): pltpu.make_async_remote_copy(
        src_ref=hidden.at[1, :, pl.ds(depth + g * group, group)],
        dst_ref=hidden.at[plane, :, pl.ds(depth + g * group, group)],
        send_sem=h_send.at[d, g], recv_sem=h_recv.at[d, g],
        device_id=(space, c), device_id_type=MESH)
        for d, _, _, space, plane in ways for g in range(GROUPS)}
    always = s >= 0
    planes = ((0, has_hi, has_lo, s_up, 0), (1, has_lo, has_hi, s_dn, 2), (2, always, always, s, 1))
    rims = ((0, c_lo, c_hi, c_dn, depth, wide - depth), (1, c_hi, c_lo, c_up, width, 0))
    to_e = {(d, t): pltpu.make_async_remote_copy(
        src_ref=hidden.at[1, :, pl.ds(src_at, depth)],
        dst_ref=hidden.at[plane, :, pl.ds(dst_at, depth)],
        send_sem=e_send.at[d, t], recv_sem=e_recv.at[d, t],
        device_id=(space, chan), device_id_type=MESH)
        for d, _, _, space, plane in planes for t, _, _, chan, src_at, dst_at in rims}

    def send_hidden(g):
        for d, sends, _, _, _ in ways:
            @pl.when(sends)
            def _(d=d):
                to_h[d, g].start()
        for t, goes, _, _, _, _ in rims:
            if g == (0, GROUPS - 1)[t]:
                for d, sends, _, _, _ in planes:
                    @pl.when(sends & goes)
                    def _(d=d, t=t):
                        to_e[d, t].start()

    def await_x(h):
        local[h].wait()
        for d, _, comes, _, _ in ways:
            @pl.when(comes)
            def _(d=d):
                for k in range(nc):
                    to_x[d, k, h].wait_recv()

    bias1 = bias[0]
    for step, g in enumerate(ORDER_ONE):
        if step == 0:
            await_x(0)
        if step == GROUPS // 2:
            await_x(1)
        layer(field, mat1, bias1, g, keep)
        send_hidden(g)

    def await_h(g):
        for d, _, comes, _, _ in ways:
            @pl.when(comes)
            def _(d=d):
                to_h[d, g].wait_recv()
        for t, _, lands, _, _, _ in rims:
            if g == (GROUPS - 1, 0)[t]:
                for d, _, comes, _, _ in planes:
                    @pl.when(comes & lands)
                    def _(d=d, t=t):
                        to_e[d, t].wait_recv()

    def piece(g):
        return pl.ds(pl.multiple_of(c * width + g * group, depth), group)

    to_o = {(k, g): pltpu.make_async_remote_copy(
        src_ref=result.at[part(peers[k]), pl.ds(g * group, group)],
        dst_ref=out.at[:, piece(g)],
        send_sem=o_send.at[k - 1, g], recv_sem=o_recv.at[k - 1, g],
        device_id=(s, peers[k]), device_id_type=MESH)
        for k in range(1, nc) for g in range(GROUPS)}
    own_o = [pltpu.make_async_copy(
        result.at[part(c), pl.ds(g * group, group)], out.at[:, piece(g)], o_local.at[g])
        for g in range(GROUPS)]

    bias2 = bias[1]
    seen = set()
    for g in ORDER_TWO:
        for near in (g - 1, g, g + 1):
            if 0 <= near < GROUPS and near not in seen:
                seen.add(near)
                await_h(near)
        layer(hidden, mat2, bias2, g, finish)
        for k in range(1, nc):
            to_o[k, g].start()
        own_o[g].start()

    for (k, h), copy in to_z.items():
        copy.wait_send()
    for d, sends, _, _, _ in ways:
        @pl.when(sends)
        def _(d=d):
            for k in range(nc):
                for h in range(2):
                    to_x[d, k, h].wait_send()
            for g in range(GROUPS):
                to_h[d, g].wait_send()
    for d, sends, _, _, _ in planes:
        for t, goes, _, _, _, _ in rims:
            @pl.when(sends & goes)
            def _(d=d, t=t):
                to_e[d, t].wait_send()
    for copy in to_o.values():
        copy.wait()
    for copy in own_o:
        copy.wait()


def per_device(volume, weight_one, bias_one, weight_two, bias_two):
    own, planes, height, depth = volume.shape
    ns, nc = lax.axis_size("space"), lax.axis_size("chan")
    rows = height // nc
    chans = own * nc
    wide = (rows + 2) * depth
    flat = jnp.pad(volume.reshape(own, height * depth), ((0, 0), (depth, depth)))
    dma = pltpu.SemaphoreType.DMA
    any_space = pl.BlockSpec(memory_space=pl.ANY)
    vmem = pl.BlockSpec(memory_space=pltpu.VMEM)
    macs = 27 * chans * chans * rows * depth
    result = pl.pallas_call(
        functools.partial(kernel, ns, nc, rows, depth, own),
        out_shape=jax.ShapeDtypeStruct((own, height * depth), BF16),
        in_specs=[any_space, any_space, vmem, any_space, vmem],
        out_specs=any_space,
        scratch_shapes=[
            pltpu.VMEM((3, chans, wide), BF16),
            pltpu.VMEM((3, chans, wide), BF16),
            pltpu.VMEM((chans, rows * depth), BF16),
            pltpu.VMEM(weight_one.shape, BF16),
            pltpu.VMEM(weight_two.shape, BF16),
            pltpu.VMEM((3 * chans, 9 * chans), BF16),
            pltpu.VMEM((3 * chans, 9 * chans), BF16),
            pltpu.VMEM((2, chans, depth), F32),
            dma((2,)), dma((2,)),
            dma((nc - 1, 2)), dma((nc - 1, 2)),
            dma((2, nc, 2)), dma((2, nc, 2)),
            dma((2, GROUPS)), dma((2, GROUPS)),
            dma((3, 2)), dma((3, 2)),
            dma((nc - 1, GROUPS)), dma((nc - 1, GROUPS)), dma((GROUPS,)),
        ],
        compiler_params=pltpu.CompilerParams(
            collective_id=0, has_side_effects=True, vmem_limit_bytes=40 * 2**20),
        cost_estimate=pl.CostEstimate(
            flops=4 * macs, bytes_accessed=4 * 2**20, transcendentals=0),
        name="conv_pair",
    )(flat, weight_one, bias_one.reshape(1, chans), weight_two, bias_two.reshape(1, chans))
    return result.reshape(own, planes, height, depth)


def solution(mesh):
    placed = (P("chan", "space", None, None), P(), P(), P(), P())
    return jax.shard_map(
        per_device,
        mesh=mesh,
        in_specs=placed,
        out_specs=P("chan", "space", None, None),
        check_vma=False,
    )
```

time: 236 us -> 48.4 us (0.21)
  waiting for transfers between devices: 167 us -> 0 us
  Pallas kernels: 0 us -> 44.4 us
  matrix products: 20 us -> 0 us
  other arithmetic: 15.7 us -> 0 us
  between operations: 13.5 us -> 0.05 us
  starting transfers between devices: 13.1 us -> 0 us
    all_gather x2 -> x0, waiting for transfers between devices: 91.2 us -> none  [per_device(): gathered = lax.all_gather(current, 'chan', axis=0, tiled=True)]
    ppermute x4 -> x0, waiting for transfers between devices: 76.1 us -> none  [the longest x2 76.1 us: extended(): before = lax.ppermute(last, axis, up)]
    pallas_call x0 -> x1, Pallas kernels: none -> 44.4 us  [per_device(): pl.pallas_call(functools.partial(kernel, ns, nc, rows, depth, own), out_s...]
    dot_general x6 -> x0, matrix products: 20 us -> none  [convolve(): jnp.einsum('tio,ixyz->toxyz', tap_weights, slab_in, preferred_element_typ...]
    convert_element_type x2 -> x0, other arithmetic: 15.7 us -> none  [per_device(): jax.nn.relu(summed + own_offsets[:, None, None, None]).astype(jnp.bfloat16)]
    ppermute x4 -> x0, starting transfers between devices: 13.1 us -> none  [the longest x2 9.26 us: extended(): after = lax.ppermute(initial, axis, down)]
  transfers between devices with their start and end apart: 6 -> 0, of which waited for: 4 -> 0; matrix products, arithmetic and copies ran while one was open for 5% -> 0% of each run, Pallas kernels for 0% -> 0%
where the time goes in v1:
time: 48.4 us; the launch traced here: 47.5 us
  Pallas kernels  44.4 us (92%)
  local copies, waits for them, and re-layouts  3.08 us (6%)
    pallas_call x1, Pallas kernels, per_device(): pl.pallas_call(functools.partial(kernel, ns, nc, rows, depth, own), out_s...  44.4 us
    unnamed x10, local copies, waits for them, and re-layouts  3.04 us

profile of v1, /device:TPU:4, one launch (start us, length us, event | category | flops | bytes accessed | tf_op | source)
XLA Modules:
  0.0 47.5 jit_solution(5550697798679818814)
XLA Ops:
  0.0 0.0 copy-start
  0.0 0.0 copy-start.1
  0.0 1.5 %copy.10 = bf16[4,8,64,128]{3,1,2,0:T(8,128)(2,1)S(1)} copy(bf16[4,8,64,128]{3,2,1,0:T(8,128)(2,1)} %bitcast.17) | data formatting | bytes 1048576
  1.5 0.0 copy-start.2
  1.5 0.0 copy-start.3
  1.6 0.0 copy-done
  1.6 0.0 copy-done.1
  1.6 0.6 %copy-done.2 = f32[128]{0:T(128)S(1)} copy-done((f32[128]{0:T(128)S(1)}, f32[128]{0:T(128)}, u32[]{:S(2)}) %copy-start.2) | copy-done | bytes 536
  2.2 0.0 copy-done.3
  2.2 44.4 %conv_pair.1 = bf16[32,8192]{1,0:T(8,128)(2,1)S(1)} custom-call(bf16[32,8448]{1,0:T(8,128)(2,1)S(1)} %pad.4.vol, bf16[27,128,128]{2,1,0:T(8,128)(2,1)S(1)} %copy-done, f32[1,128]{1,0:T(1,128)S(1)} %bitcast.14, bf16[27,128,128]{2,1,0:T(8,128)(2,1)S(1)} %copy-done.1, f32[1,128]{1,0:T(1,128)S(1)} %bitcast.15), custom_call_target="tpu_custom_call" | custom-call | flops 3623878656 | bytes 4194304 | tf_op jit(solution)/shard_map/conv_pair/pallas_call | solution.py:289
  46.6 0.9 %copy.8 = bf16[4,8,64,128]{3,2,1,0:T(8,128)(2,1)} copy(bf16[4,8,64,128]{3,1,2,0:T(8,128)(2,1)S(1)} %bitcast.13) | data formatting | bytes 1048576
  (1 shorter events, 0.0 us)
Async XLA Ops:
  0.0 1.6 %copy-start = (bf16[27,128,128]{2,1,0:T(8,128)(2,1)S(1)}, bf16[27,128,128]{2,1,0:T(8,128)(2,1)}, u32[]{:S(2)}) copy-start(bf16[27,128,128]{2,1,0:T(8,128)(2,1)} %w1.1) | copy-start | bytes 2654212
  0.0 1.6 %copy-start.1 = (bf16[27,128,128]{2,1,0:T(8,128)(2,1)S(1)}, bf16[27,128,128]{2,1,0:T(8,128)(2,1)}, u32[]{:S(2)}) copy-start(bf16[27,128,128]{2,1,0:T(8,128)(2,1)} %w2.1) | copy-start | bytes 2654212
  1.5 0.7 %copy-start.2 = (f32[128]{0:T(128)S(1)}, f32[128]{0:T(128)}, u32[]{:S(2)}) copy-start(f32[128]{0:T(128)} %param.7) | copy-start | bytes 1540
  1.5 0.7 %copy-start.3 = (f32[128]{0:T(128)S(1)}, f32[128]{0:T(128)}, u32[]{:S(2)}) copy-start(f32[128]{0:T(128)} %param.9) | copy-start | bytes 1540

commit v2 on v1

v2 whole, which is shorter than its diff:
```python
import functools

import jax
import jax.numpy as jnp
from jax import lax
from jax.experimental import pallas as pl
from jax.experimental.pallas import tpu as pltpu
from jax.sharding import PartitionSpec as P

MESH = pl.DeviceIdType.MESH
BF16 = jnp.bfloat16
F32 = jnp.float32
PAIR = 2


def row_chunks(rows):
    chunks = [(rows - 2, 4), (0, 4)]
    start = 4
    while start < rows - 2:
        size = min(6, rows - 2 - start)
        chunks.append((start, size))
        start += size
    return chunks


def kernel(ns, nc, rows, depth, own, vol, w1, b1, w2, b2, out,
           field, hidden, result, raw1, raw2, mat1, mat2, bias,
           w_sem, local_sem, z_send, z_recv, x_send, x_recv,
           h_send, h_recv, e_send, e_recv, o_send, o_recv, o_local):
    s = lax.axis_index("space")
    c = lax.axis_index("chan")
    chans = own * nc
    has_lo, has_hi = s > 0, s < ns - 1
    c_lo, c_hi = c > 0, c < nc - 1
    s_dn, s_up = jnp.maximum(s - 1, 0), jnp.minimum(s + 1, ns - 1)
    c_dn, c_up = jnp.maximum(c - 1, 0), jnp.minimum(c + 1, nc - 1)
    peers = [lax.rem(c + k, nc) for k in range(nc)]
    sources = [lax.rem(c + nc - k, nc) for k in range(nc)]
    width = rows * depth
    wide = width + 2 * depth
    groups = rows // PAIR
    group = PAIR * depth
    chunks = row_chunks(rows)
    firsts = [0, 1] + [start // PAIR for start, _ in chunks[2:]]

    load1 = pltpu.make_async_copy(w1, raw1, w_sem.at[0])
    load2 = pltpu.make_async_copy(w2, raw2, w_sem.at[1])
    load1.start()
    load2.start()

    @pl.when(s == 0)
    def _():
        field[0] = jnp.zeros((chans, wide), BF16)
        hidden[0] = jnp.zeros((chans, wide), BF16)

    @pl.when(s == ns - 1)
    def _():
        field[2] = jnp.zeros((chans, wide), BF16)
        hidden[2] = jnp.zeros((chans, wide), BF16)

    @pl.when(c == 0)
    def _():
        hidden[:, :, 0:depth] = jnp.zeros((3, chans, depth), BF16)

    @pl.when(c == nc - 1)
    def _():
        hidden[:, :, wide - depth : wide] = jnp.zeros((3, chans, depth), BF16)

    barrier = pltpu.get_barrier_semaphore()

    def greet(space, chan):
        pl.semaphore_signal(barrier, inc=1, device_id=(space, chan), device_id_type=MESH)

    for k in range(1, nc):
        greet(s, peers[k])
    for there, space in ((has_lo, s_dn), (has_hi, s_up)):
        @pl.when(there)
        def _(space=space):
            greet(space, c)

        @pl.when(there & c_lo)
        def _(space=space):
            greet(space, c_dn)

        @pl.when(there & c_hi)
        def _(space=space):
            greet(space, c_up)
    sides = has_lo.astype(jnp.int32) + has_hi.astype(jnp.int32)
    edges = c_lo.astype(jnp.int32) + c_hi.astype(jnp.int32)
    pl.semaphore_wait(barrier, nc - 1 + sides * (1 + edges))

    def part(index):
        return pl.ds(pl.multiple_of(index * own, own), own)

    def window(index, h):
        start, size = chunks[h]
        return pl.ds(pl.multiple_of(index * width + start * depth, depth), size * depth)

    def landed(h):
        start, size = chunks[h]
        return pl.ds(start * depth, size * depth)

    local = [pltpu.make_async_copy(
        vol.at[:, window(c, h)], field.at[1, part(c), landed(h)], local_sem.at[h])
        for h in range(len(chunks))]
    to_z = {(k, h): pltpu.make_async_remote_copy(
        src_ref=vol.at[:, window(peers[k], h)],
        dst_ref=field.at[1, part(c), landed(h)],
        send_sem=z_send.at[k - 1, h], recv_sem=z_recv.at[k - 1, h],
        device_id=(s, peers[k]), device_id_type=MESH)
        for h in range(len(chunks)) for k in range(1, nc)}
    ways = ((0, has_hi, has_lo, s_up, 0), (1, has_lo, has_hi, s_dn, 2))
    to_x = {}
    for d, _, _, space, plane in ways:
        for h in range(len(chunks)):
            for k in range(nc):
                if k == 0:
                    src = vol.at[:, window(c, h)]
                else:
                    src = field.at[1, part(sources[k]), landed(h)]
                to_x[d, k, h] = pltpu.make_async_remote_copy(
                    src_ref=src,
                    dst_ref=field.at[plane, part(sources[k]), landed(h)],
                    send_sem=x_send.at[d, k, h], recv_sem=x_recv.at[d, k, h],
                    device_id=(space, c), device_id_type=MESH)

    def forward(k, h):
        for d, sends, _, _, _ in ways:
            @pl.when(sends)
            def _(d=d):
                to_x[d, k, h].start()

    def begin(h):
        for k in range(1, nc):
            to_z[k, h].start()
        local[h].start()
        forward(0, h)

    def relay(h):
        for k in range(1, nc):
            to_z[k, h].wait_recv()
            forward(k, h)

    begin(0)
    begin(1)

    def turn(raw, mat, ae_range):
        for ae in ae_range:
            for f in range(3):
                mat[f * chans : (f + 1) * chans, ae * chans : (ae + 1) * chans] = raw[3 * ae + f].T

    load1.wait()
    turn(raw1, mat1, range(9))
    bias[0] = jnp.broadcast_to(b1[...], (depth, chans)).T
    bias[1] = jnp.broadcast_to(b2[...], (depth, chans)).T

    relay(0)
    begin(2)
    load2.wait()
    turn(raw2, mat2, range(3))
    relay(1)
    if len(chunks) > 3:
        begin(3)
    turn(raw2, mat2, range(3, 9))
    relay(2)

    lane = lax.broadcasted_iota(jnp.int32, (chans, depth), 1)

    def layer(source, mat, layer_bias, g, store):
        at = pl.multiple_of(g * group, group)
        stacked = jnp.concatenate(
            [source[a, :, pl.ds(pl.multiple_of(at + e * depth, depth), group)]
             for a in range(3) for e in range(3)], axis=0)
        products = jnp.dot(mat[...], stacked, preferred_element_type=F32)
        for r in range(PAIR):
            cols = slice(r * depth, (r + 1) * depth)
            left = pltpu.roll(products[0:chans, cols], 1, 1)
            right = pltpu.roll(products[2 * chans : 3 * chans, cols], depth - 1, 1)
            total = products[chans : 2 * chans, cols] + layer_bias
            total = total + jnp.where(lane == 0, 0.0, left)
            total = total + jnp.where(lane == depth - 1, 0.0, right)
            store(at + r * depth, jnp.maximum(total, 0.0).astype(BF16))

    def keep(at, value):
        hidden[1, :, pl.ds(pl.multiple_of(at + depth, depth), depth)] = value

    def finish(at, value):
        result[:, pl.ds(pl.multiple_of(at, depth), depth)] = value

    def to_h(d, g):
        space, plane = ways[d][3:]
        cols = pl.ds(pl.multiple_of(g * group + depth, depth), group)
        return pltpu.make_async_remote_copy(
            src_ref=hidden.at[1, :, cols], dst_ref=hidden.at[plane, :, cols],
            send_sem=h_send.at[d, g], recv_sem=h_recv.at[d, g],
            device_id=(space, c), device_id_type=MESH)

    always = s >= 0
    planes = ((0, has_hi, has_lo, s_up, 0), (1, has_lo, has_hi, s_dn, 2), (2, always, always, s, 1))
    rims = ((0, c_lo, c_hi, c_dn, depth, wide - depth), (1, c_hi, c_lo, c_up, width, 0))
    to_e = {(d, t): pltpu.make_async_remote_copy(
        src_ref=hidden.at[1, :, pl.ds(src_at, depth)],
        dst_ref=hidden.at[plane, :, pl.ds(dst_at, depth)],
        send_sem=e_send.at[d, t], recv_sem=e_recv.at[d, t],
        device_id=(space, chan), device_id_type=MESH)
        for d, _, _, space, plane in planes for t, _, _, chan, src_at, dst_at in rims}

    def send_edge(t):
        for d, sends, _, _, _ in planes:
            @pl.when(sends & rims[t][1])
            def _(d=d):
                to_e[d, t].start()

    def await_edge(t):
        for d, _, comes, _, _ in planes:
            @pl.when(comes & rims[t][2])
            def _(d=d):
                to_e[d, t].wait_recv()

    def await_x(h):
        local[h].wait()
        for d, _, comes, _, _ in ways:
            @pl.when(comes)
            def _(d=d):
                for k in range(nc):
                    to_x[d, k, h].wait_recv()

    @pl.loop(0, groups)
    def _(step):
        for h, first in enumerate(firsts):
            @pl.when(step == first)
            def _(h=h):
                if h == 2 and len(chunks) > 3:
                    relay(3)
                await_x(h)

        g = lax.rem(step + groups - 1, groups)
        layer(field, mat1, bias[0], g, keep)

        @pl.when(step == 0)
        def _():
            send_edge(1)

        @pl.when(step == 1)
        def _():
            send_edge(0)

        for d, sends, _, _, _ in ways:
            @pl.when(sends)
            def _(d=d):
                to_h(d, g).start()

    def await_h(g):
        for d, _, comes, _, _ in ways:
            @pl.when(comes)
            def _(d=d):
                to_h(d, g).wait_recv()

    def to_o(k, g):
        here = pl.ds(pl.multiple_of(g * group, group), group)
        there = pl.ds(pl.multiple_of(c * width + g * group, group), group)
        return pltpu.make_async_remote_copy(
            src_ref=result.at[part(peers[k]), here], dst_ref=out.at[:, there],
            send_sem=o_send.at[k - 1, g], recv_sem=o_recv.at[k - 1, g],
            device_id=(s, peers[k]), device_id_type=MESH)

    def own_o(g):
        here = pl.ds(pl.multiple_of(g * group, group), group)
        there = pl.ds(pl.multiple_of(c * width + g * group, group), group)
        return pltpu.make_async_copy(
            result.at[part(c), here], out.at[:, there], o_local.at[g])

    await_h(0)
    await_edge(1)

    @pl.loop(0, groups)
    def _(g):
        @pl.when(g < groups - 1)
        def _():
            await_h(g + 1)

        @pl.when(g == groups - 1)
        def _():
            await_edge(0)

        layer(hidden, mat2, bias[1], g, finish)
        for k in range(1, nc):
            to_o(k, g).start()
        own_o(g).start()

    for (k, h), copy in to_z.items():
        copy.wait_send()
    for d, sends, _, _, _ in ways:
        @pl.when(sends)
        def _(d=d):
            for k in range(nc):
                for h in range(len(chunks)):
                    to_x[d, k, h].wait_send()

            @pl.loop(0, groups)
            def _(g):
                to_h(d, g).wait_send()
    for d, sends, _, _, _ in planes:
        for t, goes, _, _, _, _ in rims:
            @pl.when(sends & goes)
            def _(d=d, t=t):
                to_e[d, t].wait_send()

    @pl.loop(0, groups)
    def _(g):
        for k in range(1, nc):
            to_o(k, g).wait()
        own_o(g).wait()


def per_device(volume, weight_one, bias_one, weight_two, bias_two):
    own, planes, height, depth = volume.shape
    ns, nc = lax.axis_size("space"), lax.axis_size("chan")
    rows = height // nc
    chans = own * nc
    wide = (rows + 2) * depth
    cuts = len(row_chunks(rows))
    flat = jnp.pad(volume.reshape(own, height * depth), ((0, 0), (depth, depth)))
    dma = pltpu.SemaphoreType.DMA
    any_space = pl.BlockSpec(memory_space=pl.ANY)
    vmem = pl.BlockSpec(memory_space=pltpu.VMEM)
    macs = 27 * chans * chans * rows * depth
    result = pl.pallas_call(
        functools.partial(kernel, ns, nc, rows, depth, own),
        out_shape=jax.ShapeDtypeStruct((own, height * depth), BF16),
        in_specs=[any_space, any_space, vmem, any_space, vmem],
        out_specs=any_space,
        scratch_shapes=[
            pltpu.VMEM((3, chans, wide), BF16),
            pltpu.VMEM((3, chans, wide), BF16),
            pltpu.VMEM((chans, rows * depth), BF16),
            pltpu.VMEM(weight_one.shape, BF16),
            pltpu.VMEM(weight_two.shape, BF16),
            pltpu.VMEM((3 * chans, 9 * chans), BF16),
            pltpu.VMEM((3 * chans, 9 * chans), BF16),
            pltpu.VMEM((2, chans, depth), F32),
            dma((2,)), dma((cuts,)),
            dma((nc - 1, cuts)), dma((nc - 1, cuts)),
            dma((2, nc, cuts)), dma((2, nc, cuts)),
            dma((2, rows // PAIR)), dma((2, rows // PAIR)),
            dma((3, 2)), dma((3, 2)),
            dma((nc - 1, rows // PAIR)), dma((nc - 1, rows // PAIR)), dma((rows // PAIR,)),
        ],
        compiler_params=pltpu.CompilerParams(
            collective_id=0, has_side_effects=True, vmem_limit_bytes=40 * 2**20),
        cost_estimate=pl.CostEstimate(
            flops=4 * macs, bytes_accessed=4 * 2**20, transcendentals=0),
        name="conv_pair",
    )(flat, weight_one, bias_one.reshape(1, chans), weight_two, bias_two.reshape(1, chans))
    return result.reshape(own, planes, height, depth)


def solution(mesh):
    placed = (P("chan", "space", None, None), P(), P(), P(), P())
    return jax.shard_map(
        per_device,
        mesh=mesh,
        in_specs=placed,
        out_specs=P("chan", "space", None, None),
        check_vma=False,
    )
```

time: 48.4 us -> 47.8 us (0.988)
  Pallas kernels: 44.4 us -> 43.9 us
where the time goes in v2:
time: 47.8 us; the launch traced here: 47.1 us
  Pallas kernels  43.9 us (92%)
  local copies, waits for them, and re-layouts  3.08 us (6%)
    pallas_call x1, Pallas kernels, per_device(): pl.pallas_call(functools.partial(kernel, ns, nc, rows, depth, own), out_s...  43.9 us
    unnamed x10, local copies, waits for them, and re-layouts  3.04 us

profile of v2, /device:TPU:4, one launch (start us, length us, event | category | flops | bytes accessed | tf_op | source)
XLA Modules:
  0.0 47.1 jit_solution(10811935986000144032)
XLA Ops:
  0.0 0.0 copy-start
  0.0 0.0 copy-start.1
  0.0 1.5 %copy.10 = bf16[4,8,64,128]{3,1,2,0:T(8,128)(2,1)S(1)} copy(bf16[4,8,64,128]{3,2,1,0:T(8,128)(2,1)} %bitcast.17) | data formatting | bytes 1048576
  1.5 0.0 copy-start.2
  1.5 0.0 copy-start.3
  1.6 0.0 copy-done
  1.6 0.0 copy-done.1
  1.6 0.6 %copy-done.2 = f32[128]{0:T(128)S(1)} copy-done((f32[128]{0:T(128)S(1)}, f32[128]{0:T(128)}, u32[]{:S(2)}) %copy-start.2) | copy-done | bytes 536
  2.2 0.0 copy-done.3
  2.2 43.9 %conv_pair.1 = bf16[32,8192]{1,0:T(8,128)(2,1)S(1)} custom-call(bf16[32,8448]{1,0:T(8,128)(2,1)S(1)} %pad.4.vol, bf16[27,128,128]{2,1,0:T(8,128)(2,1)S(1)} %copy-done, f32[1,128]{1,0:T(1,128)S(1)} %bitcast.14, bf16[27,128,128]{2,1,0:T(8,128)(2,1)S(1)} %copy-done.1, f32[1,128]{1,0:T(1,128)S(1)} %bitcast.15), custom_call_target="tpu_custom_call" | custom-call | flops 3623878656 | bytes 4194304 | tf_op jit(solution)/shard_map/conv_pair/pallas_call | solution.py:328
  46.2 0.9 %copy.8 = bf16[4,8,64,128]{3,2,1,0:T(8,128)(2,1)} copy(bf16[4,8,64,128]{3,1,2,0:T(8,128)(2,1)S(1)} %bitcast.13) | data formatting | bytes 1048576
  (1 shorter events, 0.0 us)
Async XLA Ops:
  0.0 1.6 %copy-start = (bf16[27,128,128]{2,1,0:T(8,128)(2,1)S(1)}, bf16[27,128,128]{2,1,0:T(8,128)(2,1)}, u32[]{:S(2)}) copy-start(bf16[27,128,128]{2,1,0:T(8,128)(2,1)} %w1.1) | copy-start | bytes 2654212
  0.0 1.6 %copy-start.1 = (bf16[27,128,128]{2,1,0:T(8,128)(2,1)S(1)}, bf16[27,128,128]{2,1,0:T(8,128)(2,1)}, u32[]{:S(2)}) copy-start(bf16[27,128,128]{2,1,0:T(8,128)(2,1)} %w2.1) | copy-start | bytes 2654212
  1.5 0.7 %copy-start.2 = (f32[128]{0:T(128)S(1)}, f32[128]{0:T(128)}, u32[]{:S(2)}) copy-start(f32[128]{0:T(128)} %param.7) | copy-start | bytes 1540
  1.5 0.7 %copy-start.3 = (f32[128]{0:T(128)S(1)}, f32[128]{0:T(128)}, u32[]{:S(2)}) copy-start(f32[128]{0:T(128)} %param.9) | copy-start | bytes 1540

commit v3 on v2

--- a/solution.py
+++ b/solution.py
@@ -225,15 +225,7 @@
                 for k in range(nc):
                     to_x[d, k, h].wait_recv()
 
-    @pl.loop(0, groups)
-    def _(step):
-        for h, first in enumerate(firsts):
-            @pl.when(step == first)
-            def _(h=h):
-                if h == 2 and len(chunks) > 3:
-                    relay(3)
-                await_x(h)
-
+    def first_layer(step):
         g = lax.rem(step + groups - 1, groups)
         layer(field, mat1, bias[0], g, keep)
 
@@ -270,11 +262,12 @@
         return pltpu.make_async_copy(
             result.at[part(c), here], out.at[:, there], o_local.at[g])
 
-    await_h(0)
-    await_edge(1)
-
-    @pl.loop(0, groups)
-    def _(g):
+    def second_layer(g):
+        @pl.when(g == 0)
+        def _():
+            await_h(0)
+            await_edge(1)
+
         @pl.when(g < groups - 1)
         def _():
             await_h(g + 1)
@@ -287,6 +280,36 @@
         for k in range(1, nc):
             to_o(k, g).start()
         own_o(g).start()
+
+    late = firsts[3] if len(chunks) > 3 else groups
+
+    @pl.loop(0, late)
+    def _(step):
+        for h in range(3):
+            @pl.when(step == firsts[h])
+            def _(h=h):
+                await_x(h)
+
+        first_layer(step)
+
+    ahead = 0
+    if len(chunks) > 3:
+        ahead = late - 3
+        relay(3)
+
+        @pl.loop(0, ahead)
+        def _(g):
+            second_layer(g)
+
+        await_x(3)
+
+        @pl.loop(late, groups)
+        def _(step):
+            first_layer(step)
+
+    @pl.loop(ahead, groups)
+    def _(g):
+        second_layer(g)
 
     for (k, h), copy in to_z.items():
         copy.wait_send()

time: 47.8 us -> 50.7 us (1.061)
  Pallas kernels: 43.9 us -> 46.6 us
    pallas_call x1, Pallas kernels: 43.9 us -> 46.6 us  [per_device(): pl.pallas_call(functools.partial(kernel, ns, nc, rows, depth, own), out_s...]
where the time goes in v3:
time: 50.7 us; the launch traced here: 49.7 us
  Pallas kernels  46.6 us (92%)
  local copies, waits for them, and re-layouts  3.08 us (6%)
    pallas_call x1, Pallas kernels, per_device(): pl.pallas_call(functools.partial(kernel, ns, nc, rows, depth, own), out_s...  46.6 us
    unnamed x10, local copies, waits for them, and re-layouts  3.04 us

profile of v3, /device:TPU:4, one launch (start us, length us, event | category | flops | bytes accessed | tf_op | source)
XLA Modules:
  0.0 49.7 jit_solution(13432520649175542086)
XLA Ops:
  0.0 0.0 copy-start
  0.0 0.0 copy-start.1
  0.0 1.5 %copy.10 = bf16[4,8,64,128]{3,1,2,0:T(8,128)(2,1)S(1)} copy(bf16[4,8,64,128]{3,2,1,0:T(8,128)(2,1)} %bitcast.17) | data formatting | bytes 1048576
  1.5 0.0 copy-start.2
  1.5 0.0 copy-start.3
  1.6 0.0 copy-done
  1.6 0.0 copy-done.1
  1.6 0.6 %copy-done.2 = f32[128]{0:T(128)S(1)} copy-done((f32[128]{0:T(128)S(1)}, f32[128]{0:T(128)}, u32[]{:S(2)}) %copy-start.2) | copy-done | bytes 536
  2.2 0.0 copy-done.3
  2.2 46.6 %conv_pair.1 = bf16[32,8192]{1,0:T(8,128)(2,1)S(1)} custom-call(bf16[32,8448]{1,0:T(8,128)(2,1)S(1)} %pad.4.vol, bf16[27,128,128]{2,1,0:T(8,128)(2,1)S(1)} %copy-done, f32[1,128]{1,0:T(1,128)S(1)} %bitcast.14, bf16[27,128,128]{2,1,0:T(8,128)(2,1)S(1)} %copy-done.1, f32[1,128]{1,0:T(1,128)S(1)} %bitcast.15), custom_call_target="tpu_custom_call" | custom-call | flops 3623878656 | bytes 4194304 | tf_op jit(solution)/shard_map/conv_pair/pallas_call | solution.py:351
  48.8 0.9 %copy.8 = bf16[4,8,64,128]{3,2,1,0:T(8,128)(2,1)} copy(bf16[4,8,64,128]{3,1,2,0:T(8,128)(2,1)S(1)} %bitcast.13) | data formatting | bytes 1048576
  (1 shorter events, 0.0 us)
Async XLA Ops:
  0.0 1.6 %copy-start = (bf16[27,128,128]{2,1,0:T(8,128)(2,1)S(1)}, bf16[27,128,128]{2,1,0:T(8,128)(2,1)}, u32[]{:S(2)}) copy-start(bf16[27,128,128]{2,1,0:T(8,128)(2,1)} %w1.1) | copy-start | bytes 2654212
  0.0 1.6 %copy-start.1 = (bf16[27,128,128]{2,1,0:T(8,128)(2,1)S(1)}, bf16[27,128,128]{2,1,0:T(8,128)(2,1)}, u32[]{:S(2)}) copy-start(bf16[27,128,128]{2,1,0:T(8,128)(2,1)} %w2.1) | copy-start | bytes 2654212
  1.5 0.7 %copy-start.2 = (f32[128]{0:T(128)S(1)}, f32[128]{0:T(128)}, u32[]{:S(2)}) copy-start(f32[128]{0:T(128)} %param.7) | copy-start | bytes 1540
  1.5 0.7 %copy-start.3 = (f32[128]{0:T(128)S(1)}, f32[128]{0:T(128)}, u32[]{:S(2)}) copy-start(f32[128]{0:T(128)} %param.9) | copy-start | bytes 1540

commit v4 on v2

--- a/solution.py
+++ b/solution.py
@@ -10,16 +10,13 @@
 MESH = pl.DeviceIdType.MESH
 BF16 = jnp.bfloat16
 F32 = jnp.float32
-PAIR = 2
+GROUP = 4
 
 
 def row_chunks(rows):
-    chunks = [(rows - 2, 4), (0, 4)]
-    start = 4
-    while start < rows - 2:
-        size = min(6, rows - 2 - start)
-        chunks.append((start, size))
-        start += size
+    chunks = [(rows - GROUP, GROUP + 2), (0, min(GROUP + 2, rows - GROUP))]
+    for start in range(GROUP + 2, rows - GROUP, GROUP):
+        chunks.append((start, min(GROUP, rows - GROUP - start)))
     return chunks
 
 
@@ -38,10 +35,10 @@
     sources = [lax.rem(c + nc - k, nc) for k in range(nc)]
     width = rows * depth
     wide = width + 2 * depth
-    groups = rows // PAIR
-    group = PAIR * depth
+    groups = rows // GROUP
+    group = GROUP * depth
     chunks = row_chunks(rows)
-    firsts = [0, 1] + [start // PAIR for start, _ in chunks[2:]]
+    firsts = list(range(len(chunks)))
 
     load1 = pltpu.make_async_copy(w1, raw1, w_sem.at[0])
     load2 = pltpu.make_async_copy(w2, raw2, w_sem.at[1])
@@ -141,8 +138,8 @@
             to_z[k, h].wait_recv()
             forward(k, h)
 
-    begin(0)
-    begin(1)
+    for h in range(len(chunks)):
+        begin(h)
 
     def turn(raw, mat, ae_range):
         for ae in ae_range:
@@ -155,14 +152,10 @@
     bias[1] = jnp.broadcast_to(b2[...], (depth, chans)).T
 
     relay(0)
-    begin(2)
     load2.wait()
     turn(raw2, mat2, range(3))
     relay(1)
-    if len(chunks) > 3:
-        begin(3)
     turn(raw2, mat2, range(3, 9))
-    relay(2)
 
     lane = lax.broadcasted_iota(jnp.int32, (chans, depth), 1)
 
@@ -172,7 +165,7 @@
             [source[a, :, pl.ds(pl.multiple_of(at + e * depth, depth), group)]
              for a in range(3) for e in range(3)], axis=0)
         products = jnp.dot(mat[...], stacked, preferred_element_type=F32)
-        for r in range(PAIR):
+        for r in range(GROUP):
             cols = slice(r * depth, (r + 1) * depth)
             left = pltpu.roll(products[0:chans, cols], 1, 1)
             right = pltpu.roll(products[2 * chans : 3 * chans, cols], depth - 1, 1)
@@ -230,8 +223,8 @@
         for h, first in enumerate(firsts):
             @pl.when(step == first)
             def _(h=h):
-                if h == 2 and len(chunks) > 3:
-                    relay(3)
+                if 0 < h < len(chunks) - 1:
+                    relay(h + 1)
                 await_x(h)
 
         g = lax.rem(step + groups - 1, groups)
@@ -342,9 +335,9 @@
             dma((2,)), dma((cuts,)),
             dma((nc - 1, cuts)), dma((nc - 1, cuts)),
             dma((2, nc, cuts)), dma((2, nc, cuts)),
-            dma((2, rows // PAIR)), dma((2, rows // PAIR)),
+            dma((2, rows // GROUP)), dma((2, rows // GROUP)),
             dma((3, 2)), dma((3, 2)),
-            dma((nc - 1, rows // PAIR)), dma((nc - 1, rows // PAIR)), dma((rows // PAIR,)),
+            dma((nc - 1, rows // GROUP)), dma((nc - 1, rows // GROUP)), dma((rows // GROUP,)),
         ],
         compiler_params=pltpu.CompilerParams(
             collective_id=0, has_side_effects=True, vmem_limit_bytes=40 * 2**20),

time: 47.8 us -> 49.8 us (1.042)
  Pallas kernels: 43.9 us -> 45.9 us
    pallas_call x1, Pallas kernels: 43.9 us -> 45.9 us  [per_device(): pl.pallas_call(functools.partial(kernel, ns, nc, rows, depth, own), out_s...]
where the time goes in v4:
time: 49.8 us; the launch traced here: 49 us
  Pallas kernels  45.9 us (92%)
  local copies, waits for them, and re-layouts  3.08 us (6%)
    pallas_call x1, Pallas kernels, per_device(): pl.pallas_call(functools.partial(kernel, ns, nc, rows, depth, own), out_s...  45.9 us
    unnamed x10, local copies, waits for them, and re-layouts  3.04 us

profile of v4, /device:TPU:4, one launch (start us, length us, event | category | flops | bytes accessed | tf_op | source)
XLA Modules:
  0.0 49.0 jit_solution(6130263190935517101)
XLA Ops:
  0.0 0.0 copy-start
  0.0 0.0 copy-start.1
  0.0 1.5 %copy.10 = bf16[4,8,64,128]{3,1,2,0:T(8,128)(2,1)S(1)} copy(bf16[4,8,64,128]{3,2,1,0:T(8,128)(2,1)} %bitcast.17) | data formatting | bytes 1048576
  1.5 0.0 copy-start.2
  1.5 0.0 copy-start.3
  1.6 0.0 copy-done
  1.6 0.0 copy-done.1
  1.6 0.6 %copy-done.2 = f32[128]{0:T(128)S(1)} copy-done((f32[128]{0:T(128)S(1)}, f32[128]{0:T(128)}, u32[]{:S(2)}) %copy-start.2) | copy-done | bytes 536
  2.2 0.0 copy-done.3
  2.2 45.9 %conv_pair.1 = bf16[32,8192]{1,0:T(8,128)(2,1)S(1)} custom-call(bf16[32,8448]{1,0:T(8,128)(2,1)S(1)} %pad.4.vol, bf16[27,128,128]{2,1,0:T(8,128)(2,1)S(1)} %copy-done, f32[1,128]{1,0:T(1,128)S(1)} %bitcast.14, bf16[27,128,128]{2,1,0:T(8,128)(2,1)S(1)} %copy-done.1, f32[1,128]{1,0:T(1,128)S(1)} %bitcast.15), custom_call_target="tpu_custom_call" | custom-call | flops 3623878656 | bytes 4194304 | tf_op jit(solution)/shard_map/conv_pair/pallas_call | solution.py:321
  48.1 0.9 %copy.8 = bf16[4,8,64,128]{3,2,1,0:T(8,128)(2,1)} copy(bf16[4,8,64,128]{3,1,2,0:T(8,128)(2,1)S(1)} %bitcast.13) | data formatting | bytes 1048576
  (1 shorter events, 0.0 us)
Async XLA Ops:
  0.0 1.6 %copy-start = (bf16[27,128,128]{2,1,0:T(8,128)(2,1)S(1)}, bf16[27,128,128]{2,1,0:T(8,128)(2,1)}, u32[]{:S(2)}) copy-start(bf16[27,128,128]{2,1,0:T(8,128)(2,1)} %w1.1) | copy-start | bytes 2654212
  0.0 1.6 %copy-start.1 = (bf16[27,128,128]{2,1,0:T(8,128)(2,1)S(1)}, bf16[27,128,128]{2,1,0:T(8,128)(2,1)}, u32[]{:S(2)}) copy-start(bf16[27,128,128]{2,1,0:T(8,128)(2,1)} %w2.1) | copy-start | bytes 2654212
  1.5 0.7 %copy-start.2 = (f32[128]{0:T(128)S(1)}, f32[128]{0:T(128)}, u32[]{:S(2)}) copy-start(f32[128]{0:T(128)} %param.7) | copy-start | bytes 1540
  1.5 0.7 %copy-start.3 = (f32[128]{0:T(128)S(1)}, f32[128]{0:T(128)}, u32[]{:S(2)}) copy-start(f32[128]{0:T(128)} %param.9) | copy-start | bytes 1540

commit v5 on v2

--- a/solution.py
+++ b/solution.py
@@ -144,25 +144,30 @@
     begin(0)
     begin(1)
 
-    def turn(raw, mat, ae_range):
-        for ae in ae_range:
+    unit = jnp.where(
+        lax.broadcasted_iota(jnp.int32, (chans, chans), 0)
+        == lax.broadcasted_iota(jnp.int32, (chans, chans), 1), 1.0, 0.0).astype(BF16)
+
+    def turn(raw, mat):
+        for ae in range(9):
+            block = raw[3 * ae : 3 * ae + 3].reshape(3 * chans, chans)
+            turned = lax.dot_general(
+                unit, block, (((1,), (1,)), ((), ())), preferred_element_type=F32).astype(BF16)
             for f in range(3):
-                mat[f * chans : (f + 1) * chans, ae * chans : (ae + 1) * chans] = raw[3 * ae + f].T
+                mat[f * chans : (f + 1) * chans, ae * chans : (ae + 1) * chans] = (
+                    turned[:, f * chans : (f + 1) * chans])
 
     load1.wait()
-    turn(raw1, mat1, range(9))
+    turn(raw1, mat1)
+    load2.wait()
+    turn(raw2, mat2)
     bias[0] = jnp.broadcast_to(b1[...], (depth, chans)).T
     bias[1] = jnp.broadcast_to(b2[...], (depth, chans)).T
 
-    relay(0)
-    begin(2)
-    load2.wait()
-    turn(raw2, mat2, range(3))
-    relay(1)
-    if len(chunks) > 3:
-        begin(3)
-    turn(raw2, mat2, range(3, 9))
-    relay(2)
+    for h in range(2):
+        relay(h)
+        if h + 2 < len(chunks):
+            begin(h + 2)
 
     lane = lax.broadcasted_iota(jnp.int32, (chans, depth), 1)
 
@@ -225,15 +230,7 @@
                 for k in range(nc):
                     to_x[d, k, h].wait_recv()
 
-    @pl.loop(0, groups)
-    def _(step):
-        for h, first in enumerate(firsts):
-            @pl.when(step == first)
-            def _(h=h):
-                if h == 2 and len(chunks) > 3:
-                    relay(3)
-                await_x(h)
-
+    def first_layer(step):
         g = lax.rem(step + groups - 1, groups)
         layer(field, mat1, bias[0], g, keep)
 
@@ -249,6 +246,28 @@
             @pl.when(sends)
             def _(d=d):
                 to_h(d, g).start()
+
+    @pl.loop(0, 2)
+    def _(step):
+        for h in range(2):
+            @pl.when(step == h)
+            def _(h=h):
+                await_x(h)
+
+        first_layer(step)
+
+    for h in range(2, len(chunks)):
+        relay(h)
+
+    @pl.loop(2, groups)
+    def _(step):
+        for h, first in enumerate(firsts):
+            if h >= 2:
+                @pl.when(step == first)
+                def _(h=h):
+                    await_x(h)
+
+        first_layer(step)
 
     def await_h(g):
         for d, _, comes, _, _ in ways:

time: 47.8 us -> 45.5 us (0.952); the launches traced: 47.1 us -> 45.3 us
  Pallas kernels: 43.9 us -> 42.2 us
    pallas_call x1, Pallas kernels: 43.9 us -> 42.2 us  [per_device(): pl.pallas_call(functools.partial(kernel, ns, nc, rows, depth, own), out_s...]
where the time goes in v5:
time: 45.5 us; the launch traced here: 45.3 us
  Pallas kernels  42.2 us (93%)
  local copies, waits for them, and re-layouts  3.08 us (7%)
    pallas_call x1, Pallas kernels, per_device(): pl.pallas_call(functools.partial(kernel, ns, nc, rows, depth, own), out_s...  42.2 us
    unnamed x10, local copies, waits for them, and re-layouts  3.04 us

profile of v5, /device:TPU:4, one launch (start us, length us, event | category | flops | bytes accessed | tf_op | source)
XLA Modules:
  0.0 45.3 jit_solution(11658883261672557564)
XLA Ops:
  0.0 0.0 copy-start
  0.0 0.0 copy-start.1
  0.0 1.5 %copy.10 = bf16[4,8,64,128]{3,1,2,0:T(8,128)(2,1)S(1)} copy(bf16[4,8,64,128]{3,2,1,0:T(8,128)(2,1)} %bitcast.17) | data formatting | bytes 1048576
  1.5 0.0 copy-start.2
  1.5 0.0 copy-start.3
  1.6 0.0 copy-done
  1.6 0.0 copy-done.1
  1.6 0.6 %copy-done.2 = f32[128]{0:T(128)S(1)} copy-done((f32[128]{0:T(128)S(1)}, f32[128]{0:T(128)}, u32[]{:S(2)}) %copy-start.2) | copy-done | bytes 536
  2.2 0.0 copy-done.3
  2.2 42.2 %conv_pair.1 = bf16[32,8192]{1,0:T(8,128)(2,1)S(1)} custom-call(bf16[32,8448]{1,0:T(8,128)(2,1)S(1)} %pad.4.vol, bf16[27,128,128]{2,1,0:T(8,128)(2,1)S(1)} %copy-done, f32[1,128]{1,0:T(1,128)S(1)} %bitcast.14, bf16[27,128,128]{2,1,0:T(8,128)(2,1)S(1)} %copy-done.1, f32[1,128]{1,0:T(1,128)S(1)} %bitcast.15), custom_call_target="tpu_custom_call" | custom-call | flops 3623878656 | bytes 4194304 | tf_op jit(solution)/shard_map/conv_pair/pallas_call | solution.py:347
  44.4 0.9 %copy.8 = bf16[4,8,64,128]{3,2,1,0:T(8,128)(2,1)} copy(bf16[4,8,64,128]{3,1,2,0:T(8,128)(2,1)S(1)} %bitcast.13) | data formatting | bytes 1048576
  (1 shorter events, 0.0 us)
Async XLA Ops:
  0.0 1.6 %copy-start = (bf16[27,128,128]{2,1,0:T(8,128)(2,1)S(1)}, bf16[27,128,128]{2,1,0:T(8,128)(2,1)}, u32[]{:S(2)}) copy-start(bf16[27,128,128]{2,1,0:T(8,128)(2,1)} %w1.1) | copy-start | bytes 2654212
  0.0 1.6 %copy-start.1 = (bf16[27,128,128]{2,1,0:T(8,128)(2,1)S(1)}, bf16[27,128,128]{2,1,0:T(8,128)(2,1)}, u32[]{:S(2)}) copy-start(bf16[27,128,128]{2,1,0:T(8,128)(2,1)} %w2.1) | copy-start | bytes 2654212
  1.5 0.7 %copy-start.2 = (f32[128]{0:T(128)S(1)}, f32[128]{0:T(128)}, u32[]{:S(2)}) copy-start(f32[128]{0:T(128)} %param.7) | copy-start | bytes 1540
  1.5 0.7 %copy-start.3 = (f32[128]{0:T(128)S(1)}, f32[128]{0:T(128)}, u32[]{:S(2)}) copy-start(f32[128]{0:T(128)} %param.9) | copy-start | bytes 1540

commit v6 on v5

--- a/solution.py
+++ b/solution.py
@@ -24,7 +24,7 @@
 
 
 def kernel(ns, nc, rows, depth, own, vol, w1, b1, w2, b2, out,
-           field, hidden, result, raw1, raw2, mat1, mat2, bias,
+           field, hidden, result, raw1, raw2, mat1, mat2, bias, raw_bias,
            w_sem, local_sem, z_send, z_recv, x_send, x_recv,
            h_send, h_recv, e_send, e_recv, o_send, o_recv, o_local):
     s = lax.axis_index("space")
@@ -45,8 +45,12 @@
 
     load1 = pltpu.make_async_copy(w1, raw1, w_sem.at[0])
     load2 = pltpu.make_async_copy(w2, raw2, w_sem.at[1])
+    load3 = pltpu.make_async_copy(b1, raw_bias.at[0], w_sem.at[2])
+    load4 = pltpu.make_async_copy(b2, raw_bias.at[1], w_sem.at[3])
     load1.start()
     load2.start()
+    load3.start()
+    load4.start()
 
     @pl.when(s == 0)
     def _():
@@ -141,8 +145,8 @@
             to_z[k, h].wait_recv()
             forward(k, h)
 
-    begin(0)
-    begin(1)
+    for h in range(len(chunks)):
+        begin(h)
 
     unit = jnp.where(
         lax.broadcasted_iota(jnp.int32, (chans, chans), 0)
@@ -161,13 +165,13 @@
     turn(raw1, mat1)
     load2.wait()
     turn(raw2, mat2)
-    bias[0] = jnp.broadcast_to(b1[...], (depth, chans)).T
-    bias[1] = jnp.broadcast_to(b2[...], (depth, chans)).T
+    load3.wait()
+    load4.wait()
+    bias[0] = jnp.broadcast_to(raw_bias[0], (depth, chans)).T
+    bias[1] = jnp.broadcast_to(raw_bias[1], (depth, chans)).T
 
     for h in range(2):
         relay(h)
-        if h + 2 < len(chunks):
-            begin(h + 2)
 
     lane = lax.broadcasted_iota(jnp.int32, (chans, depth), 1)
 
@@ -342,12 +346,11 @@
     flat = jnp.pad(volume.reshape(own, height * depth), ((0, 0), (depth, depth)))
     dma = pltpu.SemaphoreType.DMA
     any_space = pl.BlockSpec(memory_space=pl.ANY)
-    vmem = pl.BlockSpec(memory_space=pltpu.VMEM)
     macs = 27 * chans * chans * rows * depth
     result = pl.pallas_call(
         functools.partial(kernel, ns, nc, rows, depth, own),
         out_shape=jax.ShapeDtypeStruct((own, height * depth), BF16),
-        in_specs=[any_space, any_space, vmem, any_space, vmem],
+        in_specs=[any_space] * 5,
         out_specs=any_space,
         scratch_shapes=[
             pltpu.VMEM((3, chans, wide), BF16),
@@ -358,7 +361,8 @@
             pltpu.VMEM((3 * chans, 9 * chans), BF16),
             pltpu.VMEM((3 * chans, 9 * chans), BF16),
             pltpu.VMEM((2, chans, depth), F32),
-            dma((2,)), dma((cuts,)),
+            pltpu.VMEM((2, 1, chans), F32),
+            dma((4,)), dma((cuts,)),
             dma((nc - 1, cuts)), dma((nc - 1, cuts)),
             dma((2, nc, cuts)), dma((2, nc, cuts)),
             dma((2, rows // PAIR)), dma((2, rows // PAIR)),

time: 45.5 us -> 47.3 us (1.040)
  Pallas kernels: 42.2 us -> 44 us
    pallas_call x1, Pallas kernels: 42.2 us -> 44 us  [per_device(): pl.pallas_call(functools.partial(kernel, ns, nc, rows, depth, own), out_s...]
where the time goes in v6:
time: 47.3 us; the launch traced here: 47.1 us
  Pallas kernels  44 us (93%)
  local copies, waits for them, and re-layouts  3.08 us (7%)
    pallas_call x1, Pallas kernels, per_device(): pl.pallas_call(functools.partial(kernel, ns, nc, rows, depth, own), out_s...  44 us
    unnamed x10, local copies, waits for them, and re-layouts  3.04 us

profile of v6, /device:TPU:4, one launch (start us, length us, event | category | flops | bytes accessed | tf_op | source)
XLA Modules:
  0.0 47.1 jit_solution(9283141519818124789)
XLA Ops:
  0.0 0.0 copy-start
  0.0 0.0 copy-start.1
  0.0 1.5 %copy.10 = bf16[4,8,64,128]{3,1,2,0:T(8,128)(2,1)S(1)} copy(bf16[4,8,64,128]{3,2,1,0:T(8,128)(2,1)} %bitcast.17) | data formatting | bytes 1048576
  1.5 0.0 copy-start.2
  1.5 0.0 copy-start.3
  1.6 0.0 copy-done
  1.6 0.0 copy-done.1
  1.6 0.6 %copy-done.2 = f32[128]{0:T(128)S(1)} copy-done((f32[128]{0:T(128)S(1)}, f32[128]{0:T(128)}, u32[]{:S(2)}) %copy-start.2) | copy-done | bytes 536
  2.2 0.0 copy-done.3
  2.2 44.0 %conv_pair.1 = bf16[32,8192]{1,0:T(8,128)(2,1)S(1)} custom-call(bf16[32,8448]{1,0:T(8,128)(2,1)S(1)} %pad.4.vol, bf16[27,128,128]{2,1,0:T(8,128)(2,1)S(1)} %copy-done, f32[1,128]{1,0:T(1,128)S(1)} %bitcast.14, bf16[27,128,128]{2,1,0:T(8,128)(2,1)S(1)} %copy-done.1, f32[1,128]{1,0:T(1,128)S(1)} %bitcast.15), custom_call_target="tpu_custom_call" | custom-call | flops 3623878656 | bytes 4194304 | tf_op jit(solution)/shard_map/conv_pair/pallas_call | solution.py:350
  46.2 0.9 %copy.8 = bf16[4,8,64,128]{3,2,1,0:T(8,128)(2,1)} copy(bf16[4,8,64,128]{3,1,2,0:T(8,128)(2,1)S(1)} %bitcast.13) | data formatting | bytes 1048576
  (1 shorter events, 0.0 us)
Async XLA Ops:
  0.0 1.6 %copy-start = (bf16[27,128,128]{2,1,0:T(8,128)(2,1)S(1)}, bf16[27,128,128]{2,1,0:T(8,128)(2,1)}, u32[]{:S(2)}) copy-start(bf16[27,128,128]{2,1,0:T(8,128)(2,1)} %w1.1) | copy-start | bytes 2654212
  0.0 1.6 %copy-start.1 = (bf16[27,128,128]{2,1,0:T(8,128)(2,1)S(1)}, bf16[27,128,128]{2,1,0:T(8,128)(2,1)}, u32[]{:S(2)}) copy-start(bf16[27,128,128]{2,1,0:T(8,128)(2,1)} %w2.1) | copy-start | bytes 2654212
  1.5 0.7 %copy-start.2 = (f32[128]{0:T(128)S(1)}, f32[128]{0:T(128)}, u32[]{:S(2)}) copy-start(f32[128]{0:T(128)} %param.7) | copy-start | bytes 1540
  1.5 0.7 %copy-start.3 = (f32[128]{0:T(128)S(1)}, f32[128]{0:T(128)}, u32[]{:S(2)}) copy-start(f32[128]{0:T(128)} %param.9) | copy-start | bytes 1540

commit v7 on v5

--- a/solution.py
+++ b/solution.py
@@ -35,6 +35,7 @@
     s_dn, s_up = jnp.maximum(s - 1, 0), jnp.minimum(s + 1, ns - 1)
     c_dn, c_up = jnp.maximum(c - 1, 0), jnp.minimum(c + 1, nc - 1)
     peers = [lax.rem(c + k, nc) for k in range(nc)]
+    near_first = sorted(range(1, nc), key=lambda k: min(k, nc - k))
     sources = [lax.rem(c + nc - k, nc) for k in range(nc)]
     width = rows * depth
     wide = width + 2 * depth
@@ -137,7 +138,7 @@
         forward(0, h)
 
     def relay(h):
-        for k in range(1, nc):
+        for k in near_first:
             to_z[k, h].wait_recv()
             forward(k, h)
 
@@ -259,16 +260,6 @@
     for h in range(2, len(chunks)):
         relay(h)
 
-    @pl.loop(2, groups)
-    def _(step):
-        for h, first in enumerate(firsts):
-            if h >= 2:
-                @pl.when(step == first)
-                def _(h=h):
-                    await_x(h)
-
-        first_layer(step)
-
     def await_h(g):
         for d, _, comes, _, _ in ways:
             @pl.when(comes)
@@ -289,11 +280,12 @@
         return pltpu.make_async_copy(
             result.at[part(c), here], out.at[:, there], o_local.at[g])
 
-    await_h(0)
-    await_edge(1)
-
-    @pl.loop(0, groups)
-    def _(g):
+    def second_layer(g):
+        @pl.when(g == 0)
+        def _():
+            await_h(0)
+            await_edge(1)
+
         @pl.when(g < groups - 1)
         def _():
             await_h(g + 1)
@@ -306,6 +298,29 @@
         for k in range(1, nc):
             to_o(k, g).start()
         own_o(g).start()
+
+    late = firsts[-1]
+    if late > 2:
+        @pl.loop(2, late)
+        def _(step):
+            for h, first in enumerate(firsts):
+                if 2 <= h < len(chunks) - 1:
+                    @pl.when(step == first)
+                    def _(h=h):
+                        await_x(h)
+
+            first_layer(step)
+
+    await_x(len(chunks) - 1)
+
+    @pl.loop(late, groups)
+    def _(step):
+        first_layer(step)
+        second_layer(step - late)
+
+    @pl.loop(groups - late, groups)
+    def _(g):
+        second_layer(g)
 
     for (k, h), copy in to_z.items():
         copy.wait_send()

time: 45.5 us -> 46.7 us (1.026)
  Pallas kernels: 42.2 us -> 43.4 us
    pallas_call x1, Pallas kernels: 42.2 us -> 43.4 us  [per_device(): pl.pallas_call(functools.partial(kernel, ns, nc, rows, depth, own), out_s...]
where the time goes in v7:
time: 46.7 us; the launch traced here: 46.6 us
  Pallas kernels  43.4 us (93%)
  local copies, waits for them, and re-layouts  3.08 us (7%)
    pallas_call x1, Pallas kernels, per_device(): pl.pallas_call(functools.partial(kernel, ns, nc, rows, depth, own), out_s...  43.4 us
    unnamed x10, local copies, waits for them, and re-layouts  3.04 us

profile of v7, /device:TPU:4, one launch (start us, length us, event | category | flops | bytes accessed | tf_op | source)
XLA Modules:
  0.0 46.6 jit_solution(8823509203021784619)
XLA Ops:
  0.0 0.0 copy-start
  0.0 0.0 copy-start.1
  0.0 1.5 %copy.10 = bf16[4,8,64,128]{3,1,2,0:T(8,128)(2,1)S(1)} copy(bf16[4,8,64,128]{3,2,1,0:T(8,128)(2,1)} %bitcast.17) | data formatting | bytes 1048576
  1.5 0.0 copy-start.2
  1.5 0.0 copy-start.3
  1.6 0.0 copy-done
  1.6 0.0 copy-done.1
  1.6 0.6 %copy-done.2 = f32[128]{0:T(128)S(1)} copy-done((f32[128]{0:T(128)S(1)}, f32[128]{0:T(128)}, u32[]{:S(2)}) %copy-start.2) | copy-done | bytes 536
  2.2 0.0 copy-done.3
  2.2 43.4 %conv_pair.1 = bf16[32,8192]{1,0:T(8,128)(2,1)S(1)} custom-call(bf16[32,8448]{1,0:T(8,128)(2,1)S(1)} %pad.4.vol, bf16[27,128,128]{2,1,0:T(8,128)(2,1)S(1)} %copy-done, f32[1,128]{1,0:T(1,128)S(1)} %bitcast.14, bf16[27,128,128]{2,1,0:T(8,128)(2,1)S(1)} %copy-done.1, f32[1,128]{1,0:T(1,128)S(1)} %bitcast.15), custom_call_target="tpu_custom_call" | custom-call | flops 3623878656 | bytes 4194304 | tf_op jit(solution)/shard_map/conv_pair/pallas_call | solution.py:362
  45.7 0.9 %copy.8 = bf16[4,8,64,128]{3,2,1,0:T(8,128)(2,1)} copy(bf16[4,8,64,128]{3,1,2,0:T(8,128)(2,1)S(1)} %bitcast.13) | data formatting | bytes 1048576
  (1 shorter events, 0.0 us)
Async XLA Ops:
  0.0 1.6 %copy-start = (bf16[27,128,128]{2,1,0:T(8,128)(2,1)S(1)}, bf16[27,128,128]{2,1,0:T(8,128)(2,1)}, u32[]{:S(2)}) copy-start(bf16[27,128,128]{2,1,0:T(8,128)(2,1)} %w1.1) | copy-start | bytes 2654212
  0.0 1.6 %copy-start.1 = (bf16[27,128,128]{2,1,0:T(8,128)(2,1)S(1)}, bf16[27,128,128]{2,1,0:T(8,128)(2,1)}, u32[]{:S(2)}) copy-start(bf16[27,128,128]{2,1,0:T(8,128)(2,1)} %w2.1) | copy-start | bytes 2654212
  1.5 0.7 %copy-start.2 = (f32[128]{0:T(128)S(1)}, f32[128]{0:T(128)}, u32[]{:S(2)}) copy-start(f32[128]{0:T(128)} %param.7) | copy-start | bytes 1540
  1.5 0.7 %copy-start.3 = (f32[128]{0:T(128)S(1)}, f32[128]{0:T(128)}, u32[]{:S(2)}) copy-start(f32[128]{0:T(128)} %param.9) | copy-start | bytes 1540

commit v8 on v5

--- a/solution.py
+++ b/solution.py
@@ -142,7 +142,6 @@
             forward(k, h)
 
     begin(0)
-    begin(1)
 
     unit = jnp.where(
         lax.broadcasted_iota(jnp.int32, (chans, chans), 0)
@@ -159,6 +158,7 @@
 
     load1.wait()
     turn(raw1, mat1)
+    begin(1)
     load2.wait()
     turn(raw2, mat2)
     bias[0] = jnp.broadcast_to(b1[...], (depth, chans)).T

time: 45.5 us -> 45.5 us (level)
  no operation moved by 1% of the time
where the time goes in v8:
time: 45.5 us; the launch traced here: 45.3 us
  Pallas kernels  42.2 us (93%)
  local copies, waits for them, and re-layouts  3.08 us (7%)
    pallas_call x1, Pallas kernels, per_device(): pl.pallas_call(functools.partial(kernel, ns, nc, rows, depth, own), out_s...  42.2 us
    unnamed x10, local copies, waits for them, and re-layouts  3.04 us

profile of v8, /device:TPU:4, one launch (start us, length us, event | category | flops | bytes accessed | tf_op | source)
XLA Modules:
  0.0 45.3 jit_solution(11404964562506149223)
XLA Ops:
  0.0 0.0 copy-start
  0.0 0.0 copy-start.1
  0.0 1.5 %copy.10 = bf16[4,8,64,128]{3,1,2,0:T(8,128)(2,1)S(1)} copy(bf16[4,8,64,128]{3,2,1,0:T(8,128)(2,1)} %bitcast.17) | data formatting | bytes 1048576
  1.5 0.0 copy-start.2
  1.5 0.0 copy-start.3
  1.6 0.0 copy-done
  1.6 0.0 copy-done.1
  1.6 0.6 %copy-done.2 = f32[128]{0:T(128)S(1)} copy-done((f32[128]{0:T(128)S(1)}, f32[128]{0:T(128)}, u32[]{:S(2)}) %copy-start.2) | copy-done | bytes 536
  2.2 0.0 copy-done.3
  2.2 42.2 %conv_pair.1 = bf16[32,8192]{1,0:T(8,128)(2,1)S(1)} custom-call(bf16[32,8448]{1,0:T(8,128)(2,1)S(1)} %pad.4.vol, bf16[27,128,128]{2,1,0:T(8,128)(2,1)S(1)} %copy-done, f32[1,128]{1,0:T(1,128)S(1)} %bitcast.14, bf16[27,128,128]{2,1,0:T(8,128)(2,1)S(1)} %copy-done.1, f32[1,128]{1,0:T(1,128)S(1)} %bitcast.15), custom_call_target="tpu_custom_call" | custom-call | flops 3623878656 | bytes 4194304 | tf_op jit(solution)/shard_map/conv_pair/pallas_call | solution.py:347
  44.4 0.9 %copy.8 = bf16[4,8,64,128]{3,2,1,0:T(8,128)(2,1)} copy(bf16[4,8,64,128]{3,1,2,0:T(8,128)(2,1)S(1)} %bitcast.13) | data formatting | bytes 1048576
  (1 shorter events, 0.0 us)
Async XLA Ops:
  0.0 1.6 %copy-start = (bf16[27,128,128]{2,1,0:T(8,128)(2,1)S(1)}, bf16[27,128,128]{2,1,0:T(8,128)(2,1)}, u32[]{:S(2)}) copy-start(bf16[27,128,128]{2,1,0:T(8,128)(2,1)} %w1.1) | copy-start | bytes 2654212
  0.0 1.6 %copy-start.1 = (bf16[27,128,128]{2,1,0:T(8,128)(2,1)S(1)}, bf16[27,128,128]{2,1,0:T(8,128)(2,1)}, u32[]{:S(2)}) copy-start(bf16[27,128,128]{2,1,0:T(8,128)(2,1)} %w2.1) | copy-start | bytes 2654212
  1.5 0.7 %copy-start.2 = (f32[128]{0:T(128)S(1)}, f32[128]{0:T(128)}, u32[]{:S(2)}) copy-start(f32[128]{0:T(128)} %param.7) | copy-start | bytes 1540
  1.5 0.7 %copy-start.3 = (f32[128]{0:T(128)S(1)}, f32[128]{0:T(128)}, u32[]{:S(2)}) copy-start(f32[128]{0:T(128)} %param.9) | copy-start | bytes 1540

commit v9 on v5

--- a/solution.py
+++ b/solution.py
@@ -166,8 +166,8 @@
 
     for h in range(2):
         relay(h)
-        if h + 2 < len(chunks):
-            begin(h + 2)
+        if h == 0 and len(chunks) > 2:
+            begin(2)
 
     lane = lax.broadcasted_iota(jnp.int32, (chans, depth), 1)
 
@@ -253,11 +253,14 @@
             @pl.when(step == h)
             def _(h=h):
                 await_x(h)
+                if h == 0:
+                    for later in range(3, len(chunks)):
+                        begin(later)
 
         first_layer(step)
 
-    for h in range(2, len(chunks)):
-        relay(h)
+    if len(chunks) > 2:
+        relay(2)
 
     @pl.loop(2, groups)
     def _(step):
@@ -265,6 +268,8 @@
             if h >= 2:
                 @pl.when(step == first)
                 def _(h=h):
+                    if h > 2:
+                        relay(h)
                     await_x(h)
 
         first_layer(step)

time: 45.5 us -> 49.5 us (1.088)
  Pallas kernels: 42.2 us -> 46.2 us
    pallas_call x1, Pallas kernels: 42.2 us -> 46.2 us  [per_device(): pl.pallas_call(functools.partial(kernel, ns, nc, rows, depth, own), out_s...]
where the time goes in v9:
time: 49.5 us; the launch traced here: 49.4 us
  Pallas kernels  46.2 us (93%)
  local copies, waits for them, and re-layouts  3.08 us (6%)
    pallas_call x1, Pallas kernels, per_device(): pl.pallas_call(functools.partial(kernel, ns, nc, rows, depth, own), out_s...  46.2 us
    unnamed x10, local copies, waits for them, and re-layouts  3.04 us

profile of v9, /device:TPU:4, one launch (start us, length us, event | category | flops | bytes accessed | tf_op | source)
XLA Modules:
  0.0 49.4 jit_solution(17950904967460609289)
XLA Ops:
  0.0 0.0 copy-start
  0.0 0.0 copy-start.1
  0.0 1.5 %copy.10 = bf16[4,8,64,128]{3,1,2,0:T(8,128)(2,1)S(1)} copy(bf16[4,8,64,128]{3,2,1,0:T(8,128)(2,1)} %bitcast.17) | data formatting | bytes 1048576
  1.5 0.0 copy-start.2
  1.5 0.0 copy-start.3
  1.6 0.0 copy-done
  1.6 0.0 copy-done.1
  1.6 0.6 %copy-done.2 = f32[128]{0:T(128)S(1)} copy-done((f32[128]{0:T(128)S(1)}, f32[128]{0:T(128)}, u32[]{:S(2)}) %copy-start.2) | copy-done | bytes 536
  2.2 0.0 copy-done.3
  2.2 46.2 %conv_pair.1 = bf16[32,8192]{1,0:T(8,128)(2,1)S(1)} custom-call(bf16[32,8448]{1,0:T(8,128)(2,1)S(1)} %pad.4.vol, bf16[27,128,128]{2,1,0:T(8,128)(2,1)S(1)} %copy-done, f32[1,128]{1,0:T(1,128)S(1)} %bitcast.14, bf16[27,128,128]{2,1,0:T(8,128)(2,1)S(1)} %copy-done.1, f32[1,128]{1,0:T(1,128)S(1)} %bitcast.15), custom_call_target="tpu_custom_call" | custom-call | flops 3623878656 | bytes 4194304 | tf_op jit(solution)/shard_map/conv_pair/pallas_call | solution.py:352
  48.5 0.9 %copy.8 = bf16[4,8,64,128]{3,2,1,0:T(8,128)(2,1)} copy(bf16[4,8,64,128]{3,1,2,0:T(8,128)(2,1)S(1)} %bitcast.13) | data formatting | bytes 1048576
  (1 shorter events, 0.0 us)
Async XLA Ops:
  0.0 1.6 %copy-start = (bf16[27,128,128]{2,1,0:T(8,128)(2,1)S(1)}, bf16[27,128,128]{2,1,0:T(8,128)(2,1)}, u32[]{:S(2)}) copy-start(bf16[27,128,128]{2,1,0:T(8,128)(2,1)} %w1.1) | copy-start | bytes 2654212
  0.0 1.6 %copy-start.1 = (bf16[27,128,128]{2,1,0:T(8,128)(2,1)S(1)}, bf16[27,128,128]{2,1,0:T(8,128)(2,1)}, u32[]{:S(2)}) copy-start(bf16[27,128,128]{2,1,0:T(8,128)(2,1)} %w2.1) | copy-start | bytes 2654212
  1.5 0.7 %copy-start.2 = (f32[128]{0:T(128)S(1)}, f32[128]{0:T(128)}, u32[]{:S(2)}) copy-start(f32[128]{0:T(128)} %param.7) | copy-start | bytes 1540
  1.5 0.7 %copy-start.3 = (f32[128]{0:T(128)S(1)}, f32[128]{0:T(128)}, u32[]{:S(2)}) copy-start(f32[128]{0:T(128)} %param.9) | copy-start | bytes 1540

commit v10 on v6

--- a/solution.py
+++ b/solution.py
@@ -145,8 +145,8 @@
             to_z[k, h].wait_recv()
             forward(k, h)
 
-    for h in range(len(chunks)):
-        begin(h)
+    begin(0)
+    begin(1)
 
     unit = jnp.where(
         lax.broadcasted_iota(jnp.int32, (chans, chans), 0)
@@ -172,6 +172,8 @@
 
     for h in range(2):
         relay(h)
+        if h + 2 < len(chunks):
+            begin(h + 2)
 
     lane = lax.broadcasted_iota(jnp.int32, (chans, depth), 1)
 
@@ -370,7 +372,7 @@
             dma((nc - 1, rows // PAIR)), dma((nc - 1, rows // PAIR)), dma((rows // PAIR,)),
         ],
         compiler_params=pltpu.CompilerParams(
-            collective_id=0, has_side_effects=True, vmem_limit_bytes=40 * 2**20),
+            collective_id=0, has_side_effects=True, vmem_limit_bytes=60 * 2**20),
         cost_estimate=pl.CostEstimate(
             flops=4 * macs, bytes_accessed=4 * 2**20, transcendentals=0),
         name="conv_pair",

time: 47.3 us -> 46.8 us (0.989); the launches traced: 47.1 us -> 46 us
  Pallas kernels: 44 us -> 41.8 us
  local copies, waits for them, and re-layouts: 3.08 us -> 4.17 us
    pallas_call x1, Pallas kernels: 44 us -> 41.8 us  [per_device(): pl.pallas_call(functools.partial(kernel, ns, nc, rows, depth, own), out_s...]
    pad x1, local copies, waits for them, and re-layouts: 0.04 us -> 0.83 us  [per_device(): jnp.pad(volume.reshape(own, height * depth), ((0, 0), (depth, depth)))]
    unnamed x10 -> x2, local copies, waits for them, and re-layouts: 3.04 us -> 3.34 us
where the time goes in v10:
time: 46.8 us; the launch traced here: 46 us
  Pallas kernels  41.8 us (89%)
  local copies, waits for them, and re-layouts  4.17 us (9%)
    pallas_call x1, Pallas kernels, per_device(): pl.pallas_call(functools.partial(kernel, ns, nc, rows, depth, own), out_s...  41.8 us
    unnamed x2, local copies, waits for them, and re-layouts  3.34 us

profile of v10, /device:TPU:4, one launch (start us, length us, event | category | flops | bytes accessed | tf_op | source)
XLA Modules:
  0.0 46.0 jit_solution(16049361900023796676)
XLA Ops:
  0.0 1.4 %copy.10 = bf16[4,8,64,128]{3,1,2,0:T(8,128)(2,1)S(1)} copy(bf16[4,8,64,128]{3,2,1,0:T(8,128)(2,1)} %bitcast.14) | data formatting | bytes 1048576
  1.4 0.8 %pad.4.vol = bf16[32,8448]{1,0:T(8,128)(2,1)} pad(bf16[32,8192]{1,0:T(8,128)(2,1)S(1)} %bitcast.13, bf16[]{:T(256)} %constant.2.clone.1), padding=0_0x128_128 | pad | bytes 1064962 | tf_op jit(solution)/shard_map/jit(_pad)/pad | solution.py:348
  2.2 41.8 %conv_pair.1 = bf16[32,8192]{1,0:T(8,128)(2,1)} custom-call(bf16[32,8448]{1,0:T(8,128)(2,1)} %pad.4.vol, bf16[27,128,128]{2,1,0:T(8,128)(2,1)} %w1.1, f32[1,128]{1,0:T(1,128)} %bitcast.16, bf16[27,128,128]{2,1,0:T(8,128)(2,1)} %w2.1, f32[1,128]{1,0:T(1,128)} %bitcast.17), custom_call_target="tpu_custom_call" | custom-call | flops 3623878656 | bytes 4194304 | tf_op jit(solution)/shard_map/conv_pair/pallas_call | solution.py:352
  44.0 2.0 %copy.8 = bf16[4,8,64,128]{3,2,1,0:T(8,128)(2,1)} copy(bf16[4,8,64,128]{3,1,2,0:T(8,128)(2,1)} %bitcast.15) | data formatting | bytes 1048576
